TPU v7x, 32 devices: a whole 2x2x4 slice. The times are simulated.
32 devices in a mesh: groups: 2 (over y), shot: 4 (over x, core), slab: 4 (over z).
Axes of the slice: x: 2, y: 2, z: 4, core: 2. Of those that a mesh axis runs over, the one named last changes fastest.
Arguments:
- slowness: float32 [32, 192, 128], P(('groups', 'slab')), parts along dimension 0, may hold values from 0.8 to 1.25
- wave_prev: float32 [8, 16, 192, 128], P(('groups', 'shot'), 'slab'), parts along dimension 0, may hold values from -6 to 6
- wave_now: float32 [8, 16, 192, 128], P(('groups', 'shot'), 'slab'), parts along dimension 0, may hold values from -6 to 6
- memory: float32 [8, 3, 16, 192, 128], P(('groups', 'shot'), None, 'slab'), parts along dimension 0, may hold values from -6 to 6
- adjoint_now: float32 [8, 16, 192, 128], P(('groups', 'shot'), 'slab'), parts along dimension 0, may hold values from -6 to 6
- adjoint_prev: float32 [8, 16, 192, 128], P(('groups', 'shot'), 'slab'), parts along dimension 0, may hold values from -6 to 6
- wavelet: float32 [4], replicated, may hold values from -16 to 16
- src_cells: int32 [8, 64], P(('groups', 'shot')), parts along dimension 0, may hold values from 0 to 393215
- src_signs: int32 [8, 64], P(('groups', 'shot')), parts along dimension 0, may hold values from -1 to 1, as said below
- rec_cells: int32 [512], P('groups'), parts along dimension 0, may hold values from 0 to 393215
- observed: float32 [8, 4, 256], P(('groups', 'shot')), parts along dimension 0, may hold values from -6 to 6
Outputs:
- new_slowness: float32 [32, 192, 128], P(('groups', 'slab')), parts along dimension 0
- gradient: float32 [32, 192, 128], P(('groups', 'slab'), 'shot'), parts along dimension 0
There are 2 independent parts, one for each index of `groups`. A program takes and returns all parts, laid end to end along the dimension named above; an argument that names none is the same for every part. Nothing has to cross between parts.
Inputs may be any that keep to these rules, and one draw needn't show every extreme that they name: `src_signs`: each entry is -1 or +1.
All inputs are finite; a program needn't handle non-finite values.
Results may differ from a plain program's by a relative error of at most 0.0001.
Values sent between devices are 32-bit elements; how exact they have to be, the bound alone decides.
A program may use at most 64 MiB of HBM per device.

v0:
```python
import jax
import jax.numpy as jnp
from jax import lax
from jax.sharding import PartitionSpec as P

STEPS = 4


center_coef = -2.5
near_coef = 4.0 / 3.0
far_coef = -1.0 / 12.0
courant = 0.14
relax_decay = (0.3, 0.7, 0.95)
relax_weight = (0.3, 0.2, 0.1)
update_rate = 0.05
tiny_eps = 1e-06


def padded_2(block, sides, width):
    for axis, dim in sides:
        count = lax.axis_size(axis)
        forward = [(i, i + 1) for i in range(count - 1)]
        backward = [(target, source) for source, target in forward]
        low = lax.ppermute(
            lax.slice_in_dim(block, block.shape[dim] - width, None, axis=dim), axis, forward
        )
        high = lax.ppermute(lax.slice_in_dim(block, 0, width, axis=dim), axis, backward)
        block = jnp.concatenate([low, block, high], axis=dim)
    return block


def laplace(padded):
    middle = padded[2:-2]
    flanks = jnp.pad(middle, ((0, 0), (2, 2), (2, 2)))
    depth_sum = near_coef * (padded[3:-1] + padded[1:-3]) + far_coef * (padded[4:] + padded[:-4])
    cross_sum = near_coef * (flanks[:, 3:-1, 2:-2] + flanks[:, 1:-3, 2:-2]) + far_coef * (
        flanks[:, 4:, 2:-2] + flanks[:, :-4, 2:-2]
    )
    along_sum = near_coef * (flanks[:, 2:-2, 3:-1] + flanks[:, 2:-2, 1:-3]) + far_coef * (
        flanks[:, 2:-2, 4:] + flanks[:, 2:-2, :-4]
    )
    return 3.0 * center_coef * middle + depth_sum + cross_sum + along_sum


def place_sources(cells, signs, start, count):
    local = cells - start
    inside = (local >= 0) & (local < count)
    slot = jnp.where(inside, local, count)
    return jnp.zeros((count,), jnp.float32).at[slot].add(signs.astype(jnp.float32), mode="drop")


def per_device(
    slowness,
    wave_prev,
    wave_now,
    memory,
    adjoint_now,
    adjoint_prev,
    wavelet,
    src_cells,
    src_signs,
    rec_cells,
    observed,
):
    depth, width, lanes = slowness.shape
    plane = width * lanes
    block = depth * plane
    offset = lax.axis_index("slab") * block
    decay = jnp.array(relax_decay, jnp.float32)[:, None, None, None]
    weight = jnp.array(relax_weight, jnp.float32)[:, None, None, None]
    rec_local = rec_cells - offset
    rec_inside = (rec_local >= 0) & (rec_local < block)
    rec_slot = jnp.where(rec_inside, rec_local, block)
    rec_safe = jnp.minimum(rec_slot, block - 1)
    scaled = courant / (slowness * slowness)
    older, current, relax = (wave_prev[0], wave_now[0], memory[0])
    saved = []
    misfits = []

    def record(field, level):
        picked = field.reshape(-1)[rec_safe]
        misfits.append(jnp.where(rec_inside, picked - observed[0, level], 0.0))

    src_field = place_sources(src_cells[0], src_signs[0], offset, block).reshape(
        depth, width, lanes
    )
    for level in range(STEPS):
        padded = padded_2(current, (("slab", 0),), 2)
        curved = laplace(padded)
        accel = curved + jnp.sum(relax, 0)
        newer = 2.0 * current - older + scaled * accel + wavelet[level] * src_field
        relax = decay * relax - weight * curved[None]
        older, current = (current, newer)
        saved.append(accel)
        record(current, level)
    back_prev, back_now = (adjoint_prev[0], adjoint_now[0])
    back_relax = jnp.zeros_like(relax)
    accum = jnp.zeros_like(slowness)
    for level in reversed(range(STEPS)):
        inject = (
            jnp.zeros((block,), jnp.float32)
            .at[rec_slot]
            .add(misfits[level], mode="drop")
            .reshape(depth, width, lanes)
        )
        united = back_now + inject
        pushed = scaled * united
        drive = pushed - jnp.sum(weight * back_relax, 0)
        padded = padded_2(drive, (("slab", 0),), 2)
        accum = accum + united * saved[level]
        back_prev, back_now = (-united, back_prev + 2.0 * united + laplace(padded))
        back_relax = decay * back_relax + pushed[None]
    local_grad = accum * (-2.0 * courant / (slowness * slowness * slowness))
    cells_all = lax.axis_size("slab") * block
    share = width // lax.axis_size("shot")
    first = lax.axis_index("shot") * share
    summed = lax.psum(local_grad, "shot")
    squares = lax.psum(jnp.sum(summed * summed), "slab")
    rms_value = jnp.sqrt(squares / cells_all + tiny_eps)
    normed = summed / rms_value
    new_slowness = slowness - update_rate * normed
    gradient = lax.dynamic_slice_in_dim(normed, first, share, 1)
    return (new_slowness, gradient)


def solution(mesh):
    in_specs = (
        P(("groups", "slab"), None, None),
        P(("groups", "shot"), "slab", None, None),
        P(("groups", "shot"), "slab", None, None),
        P(("groups", "shot"), None, "slab", None, None),
        P(("groups", "shot"), "slab", None, None),
        P(("groups", "shot"), "slab", None, None),
        P(),
        P(("groups", "shot"), None),
        P(("groups", "shot"), None),
        P("groups"),
        P(("groups", "shot"), None, None),
    )
    out_specs = (P(("groups", "slab"), None, None), P(("groups", "slab"), "shot", None))
    return jax.shard_map(
        per_device, mesh=mesh, in_specs=in_specs, out_specs=out_specs, check_vma=False
    )
```

profile of v0, /device:TPU:0, one launch (start us, length us, event | category | flops | bytes accessed | tf_op | source)
XLA Modules:
  0.0 166.8 jit_solution(11458838551574252018)
XLA Ops:
  9.6 5.6 %collective-permute-start.1 = (f32[2,192,128]{2,1,0:T(8,128)S(1)}, f32[2,192,128]{2,1,0:T(8,128)S(1)}, u32[]{:S(2)}, u32[]{:S(2)}) collective-permute-start(f32[2,192,128]{2,1,0:T(8,128)S(1)} %get-tuple-element.43), channel_id=1, source_target_pairs={{0,1},{1,2},{2,3},{4,5},{5,6},{6,7},{8,9},{9,10},{10,11},{12,13},{... | collective-permute-start | bytes 589832 | tf_op jit(solution)/shard_map/ppermute | solution.py:24
  20.4 2.6 %broadcast_multiply_fusion.1 = (f32[98304]{0:T(1024)S(1)}, f32[98304]{0:T(1024)S(1)}, f32[98304]{0:T(1024)S(1)}, f32[98304]{0:T(1024)S(1)}) fusion(f32[98304]{0:T(1024)S(1)} %scatter_custom_fusion, f32[]{:T(128)} %bitcast.13, f32[]{:T(128)} %bitcast.15, f32[]{:T(128)} %bitcast.11, f32[]{:T(128)} %bitcast.5), kind=kLoop, calls=%fused_computation.281 | loop fusion | flops 393216 | bytes 1966096 | tf_op jit(solution)/shard_map/mul | solution.py:91
  25.8 4.6 %collective-permute-start.3 = (f32[2,192,128]{2,1,0:T(8,128)S(1)}, f32[2,192,128]{2,1,0:T(8,128)S(1)}, u32[]{:S(2)}, u32[]{:S(2)}) collective-permute-start(f32[2,192,128]{2,1,0:T(8,128)S(1)} %get-tuple-element.41), channel_id=1, source_target_pairs={{0,1},{1,2},{2,3},{4,5},{5,6},{6,7},{8,9},{9,10},{10,11},{12,13},{... | collective-permute-start | bytes 589832 | tf_op jit(solution)/shard_map/ppermute | solution.py:24
  30.6 2.1 %collective-permute-done.2 = f32[2,192,128]{2,1,0:T(8,128)S(1)} collective-permute-done((f32[2,192,128]{2,1,0:T(8,128)S(1)}, f32[2,192,128]{2,1,0:T(8,128)S(1)}, u32[]{:S(2)}, u32[]{:S(2)}) %collective-permute-start.2) | collective-permute-done | bytes 196640 | tf_op jit(solution)/shard_map/ppermute | solution.py:27
  35.8 5.0 %collective-permute-start.5 = (f32[2,192,128]{2,1,0:T(8,128)S(1)}, f32[2,192,128]{2,1,0:T(8,128)S(1)}, u32[]{:S(2)}, u32[]{:S(2)}) collective-permute-start(f32[2,192,128]{2,1,0:T(8,128)S(1)} %get-tuple-element.35), channel_id=1, source_target_pairs={{0,1},{1,2},{2,3},{4,5},{5,6},{6,7},{8,9},{9,10},{10,11},{12,13},{... | collective-permute-start | bytes 589832 | tf_op jit(solution)/shard_map/ppermute | solution.py:24
  47.2 5.0 %collective-permute-start.7 = (f32[2,192,128]{2,1,0:T(8,128)}, f32[2,192,128]{2,1,0:T(8,128)S(1)}, u32[]{:S(2)}, u32[]{:S(2)}) collective-permute-start(f32[2,192,128]{2,1,0:T(8,128)} %get-tuple-element.33), channel_id=1, source_target_pairs={{0,1},{1,2},{2,3},{4,5},{5,6},{6,7},{8,9},{9,10},{10,11},{12,13},{... | collective-permute-start | bytes 589832 | tf_op jit(solution)/shard_map/ppermute | solution.py:24
  52.8 2.3 %gather_fusion.3 = f32[256]{0:T(256)} fusion(f32[98304]{0:T(1024)S(1)} %bitcast.58, s32[1024]{0:T(1024)S(1)} %pad_clamp_fusion), kind=kCustom, calls=%fused_computation.3 | custom fusion | bytes 3072 | tf_op jit(solution)/shard_map/gather | solution.py:81
  55.2 2.3 %gather_fusion.2 = f32[256]{0:T(256)} fusion(f32[98304]{0:T(1024)S(1)} %bitcast.57, s32[1024]{0:T(1024)S(1)} %pad_clamp_fusion), kind=kCustom, calls=%fused_computation.2 | custom fusion | bytes 3072 | tf_op jit(solution)/shard_map/gather | solution.py:81
  57.4 2.3 %gather_fusion.1 = f32[256]{0:T(256)} fusion(f32[98304]{0:T(1024)S(1)} %bitcast.59, s32[1024]{0:T(1024)S(1)} %pad_clamp_fusion), kind=kCustom, calls=%fused_computation.1 | custom fusion | bytes 3072 | tf_op jit(solution)/shard_map/gather | solution.py:81
  60.5 1.6 add_add_fusion
  62.2 1.7 %gather_fusion = f32[256]{0:T(256)S(1)} fusion(f32[98304]{0:T(1024)S(1)} %bitcast.61, s32[1024]{0:T(1024)S(1)} %pad_clamp_fusion), kind=kCustom, calls=%fused_computation | custom fusion | bytes 3072 | tf_op jit(solution)/shard_map/gather | solution.py:81
  65.2 2.2 %scatter_custom_fusion.1 = f32[98304]{0:T(1024)S(1)} fusion(s32[256]{0:T(256)} %compare_select_fusion.1, f32[256]{0:T(256)S(1)} %get-tuple-element.51, f32[]{:T(128)} %constant.19.clone.1), kind=kCustom, calls=%fused_computation.292 | custom fusion | flops 256 | bytes 393728 | tf_op jit(solution)/shard_map/scatter-add | solution.py:103
  69.5 4.6 %collective-permute-start.9 = (f32[2,192,128]{2,1,0:T(8,128)}, f32[2,192,128]{2,1,0:T(8,128)S(1)}, u32[]{:S(2)}, u32[]{:S(2)}) collective-permute-start(f32[2,192,128]{2,1,0:T(8,128)} %get-tuple-element.31), channel_id=1, source_target_pairs={{0,1},{1,2},{2,3},{4,5},{5,6},{6,7},{8,9},{9,10},{10,11},{12,13},{... | collective-permute-start | bytes 589832 | tf_op jit(solution)/shard_map/ppermute | solution.py:24
  74.1 2.2 %scatter_custom_fusion.2 = f32[98304]{0:T(1024)S(1)} fusion(s32[256]{0:T(256)} %compare_select_fusion.1, f32[256]{0:T(256)} %get-tuple-element.50, f32[]{:T(128)} %constant.19.clone.1), kind=kCustom, calls=%fused_computation.290 | custom fusion | flops 256 | bytes 393728 | tf_op jit(solution)/shard_map/scatter-add | solution.py:103
  82.4 4.9 %collective-permute-start.11 = (f32[2,192,128]{2,1,0:T(8,128)S(1)}, f32[2,192,128]{2,1,0:T(8,128)S(1)}, u32[]{:S(2)}, u32[]{:S(2)}) collective-permute-start(f32[2,192,128]{2,1,0:T(8,128)S(1)} %get-tuple-element.29), channel_id=1, source_target_pairs={{0,1},{1,2},{2,3},{4,5},{5,6},{6,7},{8,9},{9,10},{10,11},{12,13},{... | collective-permute-start | bytes 589832 | tf_op jit(solution)/shard_map/ppermute | solution.py:24
  87.3 2.8 %scatter_custom_fusion.3 = f32[98304]{0:T(1024)} fusion(s32[256]{0:T(256)} %compare_select_fusion.1, f32[256]{0:T(256)} %get-tuple-element.48, f32[]{:T(128)} %constant.19.clone.1), kind=kCustom, calls=%fused_computation.288 | custom fusion | flops 256 | bytes 393728 | tf_op jit(solution)/shard_map/scatter-add | solution.py:103
  91.2 1.8 %multiply_subtract_fusion.2 = (f32[4,192,128]{2,1,0:T(8,128)S(1)}, f32[4,192,128]{2,1,0:T(8,128)S(1)}) fusion(f32[4,192,128]{2,1,0:T(8,128)} %get-tuple-element.5, f32[4,192,128]{2,1,0:T(8,128)S(1)} %copy-done, f32[4,192,128]{2,1,0:T(8,128)} %bitcast.66, f32[4,192,128]{2,1,0:T(8,128)S(1)} %fusion.169, f32[2,192,128]{2,1,0:T(8,128)} %copy-done.10, ...), kind=kLoop, calls=%fused_computation.275 | loop fusion | flops 3145728 | bytes 3538944 | tf_op jit(solution)/shard_map/sub | solution.py:108
  95.0 5.7 %collective-permute-start.13 = (f32[2,192,128]{2,1,0:T(8,128)}, f32[2,192,128]{2,1,0:T(8,128)}, u32[]{:S(2)}, u32[]{:S(2)}) collective-permute-start(f32[2,192,128]{2,1,0:T(8,128)} %get-tuple-element.27), channel_id=1, source_target_pairs={{0,1},{1,2},{2,3},{4,5},{5,6},{6,7},{8,9},{9,10},{10,11},{12,13},{... | collective-permute-start | bytes 589832 | tf_op jit(solution)/shard_map/ppermute | solution.py:24
  100.7 2.2 %scatter_custom_fusion.4 = f32[98304]{0:T(1024)S(1)} fusion(s32[256]{0:T(256)} %compare_select_fusion.1, f32[256]{0:T(256)S(1)} %get-tuple-element.49, f32[]{:T(128)} %constant.19.clone.1), kind=kCustom, calls=%fused_computation.286 | custom fusion | flops 256 | bytes 393728 | tf_op jit(solution)/shard_map/scatter-add | solution.py:103
  103.6 2.6 %fusion.4 = f32[4,192,128]{2,1,0:T(8,128)} fusion(f32[4,192,128]{2,1,0:T(8,128)S(1)} %copy-done, f32[4,192,128]{2,1,0:T(8,128)} %get-tuple-element.24, f32[4,192,128]{2,1,0:T(8,128)S(1)} %bitcast.65, f32[2,192,128]{2,1,0:T(8,128)} %collective-permute-done.13, f32[4,192,128]{2,1,0:T(8,128)S(1)} %get-tuple-element.8, ...), kind=kLoop, calls=%fused_computation.104 | loop fusion | flops 3833856 | bytes 4718592 | tf_op jit(solution)/shard_map/mul | solution.py:113
  106.2 36.6 %all-reduce.9.cloned.1.call-done = f32[4,192,128]{2,1,0:T(8,128)} async-done(((f32[4,192,128]{2,1,0:T(8,128)}), f32[4,192,128]{2,1,0:T(8,128)}) %all-reduce.9.cloned.1.call-update) | async-done | bytes 393232 | tf_op jit(solution)/shard_map/psum | solution.py:117
  142.8 1.7 %multiply_reduce_fusion.2 = f32[]{:T(128)} fusion(f32[4,192,128]{2,1,0:T(8,128)} %all-reduce.9.cloned.1.call-done), kind=kLoop, calls=%fused_computation.274 | loop fusion | flops 196607 | bytes 393220 | tf_op jit(solution)/shard_map/reduce_sum | solution.py:118
  144.5 12.3 %psum.15 = f32[]{:T(128)} all-reduce(f32[]{:T(128)} %multiply_reduce_fusion.2), channel_id=1, replica_groups=mesh['groups'=2,'shot'=4,'slab'=4] {'slab'}, use_global_device_ids=true, to_apply=%region_14.15 | all-reduce | flops 1 | bytes 8 | tf_op jit(solution)/shard_map/psum | solution.py:118
  157.5 1.8 %multiply_subtract_fusion.1 = (f32[4,192,128]{2,1,0:T(8,128)}, f32[4,192,128]{2,1,0:T(8,128)S(1)}) fusion(f32[4,192,128]{2,1,0:T(8,128)S(1)} %copy-done, f32[4,192,128]{2,1,0:T(8,128)} %all-reduce.9.cloned.1.call-done, f32[]{:T(128)S(6)} %sqrt.3), kind=kLoop, calls=%fused_computation.273 | loop fusion | flops 294912 | bytes 1572868 | tf_op jit(solution)/shard_map/sub | solution.py:121
  (84 shorter events, 35.0 us)
Async XLA Ops:
  7.2 135.6 %all-reduce.9.cloned.1.call-start = ((), (), s32[]{:S(2)}) async-start(), calls=%async_computation | async-start | bytes 786432 | tf_op jit(solution)/shard_map/psum | solution.py:117
  8.3 14.8 %collective-permute-start = (f32[2,192,128]{2,1,0:T(8,128)S(1)}, f32[2,192,128]{2,1,0:T(8,128)S(1)}, u32[]{:S(2)}, u32[]{:S(2)}) collective-permute-start(f32[2,192,128]{2,1,0:T(8,128)S(1)} %get-tuple-element.42), channel_id=1, source_target_pairs={{1,0},{2,1},{3,2},{5,4},{6,5},{7,6},{9,8},{10,9},{11,10},{13,12},{... | collective-permute-start | bytes 589832 | tf_op jit(solution)/shard_map/ppermute | solution.py:27
  9.6 13.5 %collective-permute-start.1 = (f32[2,192,128]{2,1,0:T(8,128)S(1)}, f32[2,192,128]{2,1,0:T(8,128)S(1)}, u32[]{:S(2)}, u32[]{:S(2)}) collective-permute-start(f32[2,192,128]{2,1,0:T(8,128)S(1)} %get-tuple-element.43), channel_id=1, source_target_pairs={{0,1},{1,2},{2,3},{4,5},{5,6},{6,7},{8,9},{9,10},{10,11},{12,13},{... | collective-permute-start | bytes 589832 | tf_op jit(solution)/shard_map/ppermute | solution.py:24
  19.3 3.8 %copy-start = (f32[4,192,128]{2,1,0:T(8,128)S(1)}, f32[4,192,128]{2,1,0:T(8,128)}, u32[]{:S(2)}) copy-start(f32[4,192,128]{2,1,0:T(8,128)} %param.13) | copy-start | bytes 1179652
  19.3 3.8 %copy-start.2 = (f32[1,4,192,128]{3,2,1,0:T(8,128)S(1)}, f32[1,4,192,128]{3,2,1,0:T(8,128)}, u32[]{:S(2)}) copy-start(f32[1,4,192,128]{3,2,1,0:T(8,128)} %param.15) | copy-start | bytes 1179652
  23.1 7.2 %copy-start.1 = (f32[1,3,4,192,128]{4,3,2,1,0:T(8,128)S(1)}, f32[1,3,4,192,128]{4,3,2,1,0:T(8,128)}, u32[]{:S(2)}) copy-start(f32[1,3,4,192,128]{4,3,2,1,0:T(8,128)} %param.16) | copy-start | bytes 3538948
  23.1 7.2 %copy-start.12 = (f32[3]{0:T(128)S(1)}, f32[3]{0:T(128)}, u32[]{:S(2)}) copy-start(f32[3]{0:T(128)} %constant.18.clone) | copy-start | bytes 40
  23.1 7.2 %copy-start.13 = (f32[3]{0:T(128)S(1)}, f32[3]{0:T(128)}, u32[]{:S(2)}) copy-start(f32[3]{0:T(128)} %constant.50.clone) | copy-start | bytes 40
  24.5 8.3 %collective-permute-start.2 = (f32[2,192,128]{2,1,0:T(8,128)S(1)}, f32[2,192,128]{2,1,0:T(8,128)S(1)}, u32[]{:S(2)}, u32[]{:S(2)}) collective-permute-start(f32[2,192,128]{2,1,0:T(8,128)S(1)} %get-tuple-element.40), channel_id=1, source_target_pairs={{1,0},{2,1},{3,2},{5,4},{6,5},{7,6},{9,8},{10,9},{11,10},{13,12},{... | collective-permute-start | bytes 589832 | tf_op jit(solution)/shard_map/ppermute | solution.py:27
  25.8 8.1 %collective-permute-start.3 = (f32[2,192,128]{2,1,0:T(8,128)S(1)}, f32[2,192,128]{2,1,0:T(8,128)S(1)}, u32[]{:S(2)}, u32[]{:S(2)}) collective-permute-start(f32[2,192,128]{2,1,0:T(8,128)S(1)} %get-tuple-element.41), channel_id=1, source_target_pairs={{0,1},{1,2},{2,3},{4,5},{5,6},{6,7},{8,9},{9,10},{10,11},{12,13},{... | collective-permute-start | bytes 589832 | tf_op jit(solution)/shard_map/ppermute | solution.py:24
  33.9 6.9 %copy-start.16 = (f32[1,4,256]{2,1,0:T(4,128)S(1)}, f32[1,4,256]{2,1,0:T(4,128)}, u32[]{:S(2)}) copy-start(f32[1,4,256]{2,1,0:T(4,128)} %param.23) | copy-start | bytes 12292
  34.5 8.0 %collective-permute-start.4 = (f32[2,192,128]{2,1,0:T(8,128)S(1)}, f32[2,192,128]{2,1,0:T(8,128)S(1)}, u32[]{:S(2)}, u32[]{:S(2)}) collective-permute-start(f32[2,192,128]{2,1,0:T(8,128)S(1)} %get-tuple-element.34), channel_id=1, source_target_pairs={{1,0},{2,1},{3,2},{5,4},{6,5},{7,6},{9,8},{10,9},{11,10},{13,12},{... | collective-permute-start | bytes 589832 | tf_op jit(solution)/shard_map/ppermute | solution.py:27
  35.8 8.2 %collective-permute-start.5 = (f32[2,192,128]{2,1,0:T(8,128)S(1)}, f32[2,192,128]{2,1,0:T(8,128)S(1)}, u32[]{:S(2)}, u32[]{:S(2)}) collective-permute-start(f32[2,192,128]{2,1,0:T(8,128)S(1)} %get-tuple-element.35), channel_id=1, source_target_pairs={{0,1},{1,2},{2,3},{4,5},{5,6},{6,7},{8,9},{9,10},{10,11},{12,13},{... | collective-permute-start | bytes 589832 | tf_op jit(solution)/shard_map/ppermute | solution.py:24
  45.0 7.3 %copy-start.15 = (s32[256]{0:T(256)S(1)}, s32[256]{0:T(256)}, u32[]{:S(2)}) copy-start(s32[256]{0:T(256)} %param.22) | copy-start | bytes 3076
  45.9 13.8 %collective-permute-start.6 = (f32[2,192,128]{2,1,0:T(8,128)}, f32[2,192,128]{2,1,0:T(8,128)S(1)}, u32[]{:S(2)}, u32[]{:S(2)}) collective-permute-start(f32[2,192,128]{2,1,0:T(8,128)} %get-tuple-element.32), channel_id=1, source_target_pairs={{1,0},{2,1},{3,2},{5,4},{6,5},{7,6},{9,8},{10,9},{11,10},{13,12},{... | collective-permute-start | bytes 589832 | tf_op jit(solution)/shard_map/ppermute | solution.py:27
  47.2 12.5 %collective-permute-start.7 = (f32[2,192,128]{2,1,0:T(8,128)}, f32[2,192,128]{2,1,0:T(8,128)S(1)}, u32[]{:S(2)}, u32[]{:S(2)}) collective-permute-start(f32[2,192,128]{2,1,0:T(8,128)} %get-tuple-element.33), channel_id=1, source_target_pairs={{0,1},{1,2},{2,3},{4,5},{5,6},{6,7},{8,9},{9,10},{10,11},{12,13},{... | collective-permute-start | bytes 589832 | tf_op jit(solution)/shard_map/ppermute | solution.py:24
  62.1 5.2 %copy-start.4 = (f32[1,4,192,128]{3,2,1,0:T(8,128)S(1)}, f32[1,4,192,128]{3,2,1,0:T(8,128)}, u32[]{:S(2)}) copy-start(f32[1,4,192,128]{3,2,1,0:T(8,128)} %param.17) | copy-start | bytes 1179652
  67.4 10.9 %copy-start.3 = (f32[1,4,192,128]{3,2,1,0:T(8,128)S(1)}, f32[1,4,192,128]{3,2,1,0:T(8,128)}, u32[]{:S(2)}) copy-start(f32[1,4,192,128]{3,2,1,0:T(8,128)} %param.18) | copy-start | bytes 1179652
  68.2 8.1 %collective-permute-start.8 = (f32[2,192,128]{2,1,0:T(8,128)}, f32[2,192,128]{2,1,0:T(8,128)S(1)}, u32[]{:S(2)}, u32[]{:S(2)}) collective-permute-start(f32[2,192,128]{2,1,0:T(8,128)} %get-tuple-element.30), channel_id=1, source_target_pairs={{1,0},{2,1},{3,2},{5,4},{6,5},{7,6},{9,8},{10,9},{11,10},{13,12},{... | collective-permute-start | bytes 589832 | tf_op jit(solution)/shard_map/ppermute | solution.py:27
  69.5 8.0 %collective-permute-start.9 = (f32[2,192,128]{2,1,0:T(8,128)}, f32[2,192,128]{2,1,0:T(8,128)S(1)}, u32[]{:S(2)}, u32[]{:S(2)}) collective-permute-start(f32[2,192,128]{2,1,0:T(8,128)} %get-tuple-element.31), channel_id=1, source_target_pairs={{0,1},{1,2},{2,3},{4,5},{5,6},{6,7},{8,9},{9,10},{10,11},{12,13},{... | collective-permute-start | bytes 589832 | tf_op jit(solution)/shard_map/ppermute | solution.py:24
  81.1 9.1 %collective-permute-start.10 = (f32[2,192,128]{2,1,0:T(8,128)S(1)}, f32[2,192,128]{2,1,0:T(8,128)S(1)}, u32[]{:S(2)}, u32[]{:S(2)}) collective-permute-start(f32[2,192,128]{2,1,0:T(8,128)S(1)} %get-tuple-element.28), channel_id=1, source_target_pairs={{1,0},{2,1},{3,2},{5,4},{6,5},{7,6},{9,8},{10,9},{11,10},{13,12},{... | collective-permute-start | bytes 589832 | tf_op jit(solution)/shard_map/ppermute | solution.py:27
  82.4 8.1 %collective-permute-start.11 = (f32[2,192,128]{2,1,0:T(8,128)S(1)}, f32[2,192,128]{2,1,0:T(8,128)S(1)}, u32[]{:S(2)}, u32[]{:S(2)}) collective-permute-start(f32[2,192,128]{2,1,0:T(8,128)S(1)} %get-tuple-element.29), channel_id=1, source_target_pairs={{0,1},{1,2},{2,3},{4,5},{5,6},{6,7},{8,9},{9,10},{10,11},{12,13},{... | collective-permute-start | bytes 589832 | tf_op jit(solution)/shard_map/ppermute | solution.py:24
  93.8 9.2 %collective-permute-start.12 = (f32[2,192,128]{2,1,0:T(8,128)}, f32[2,192,128]{2,1,0:T(8,128)}, u32[]{:S(2)}, u32[]{:S(2)}) collective-permute-start(f32[2,192,128]{2,1,0:T(8,128)} %get-tuple-element.26), channel_id=1, source_target_pairs={{1,0},{2,1},{3,2},{5,4},{6,5},{7,6},{9,8},{10,9},{11,10},{13,12},{... | collective-permute-start | bytes 589832 | tf_op jit(solution)/shard_map/ppermute | solution.py:27
  95.0 8.5 %collective-permute-start.13 = (f32[2,192,128]{2,1,0:T(8,128)}, f32[2,192,128]{2,1,0:T(8,128)}, u32[]{:S(2)}, u32[]{:S(2)}) collective-permute-start(f32[2,192,128]{2,1,0:T(8,128)} %get-tuple-element.27), channel_id=1, source_target_pairs={{0,1},{1,2},{2,3},{4,5},{5,6},{6,7},{8,9},{9,10},{10,11},{12,13},{... | collective-permute-start | bytes 589832 | tf_op jit(solution)/shard_map/ppermute | solution.py:24
  (8 other events, 12.2 us)
Sparse Core Ops, SparseCore 0:
  106.3 36.4 all-reduce.8
where the time goes:
time: 168 us; the launch traced here: 167 us
  waiting for transfers between devices  44.7 us (27%)
  starting transfers between devices  44.4 us (26%)
  other arithmetic  33.3 us (20%)
  local copies, waits for them, and re-layouts  17 us (10%)
  between operations  15.2 us (9%)
  blocking collectives  12.3 us (7%)
    psum x1, waiting for transfers between devices, per_device(): summed = lax.psum(local_grad, 'shot')  36.6 us
    ppermute x7, starting transfers between devices, padded_2(): lax.ppermute(lax.slice_in_dim(block, block.shape[dim] - width, None, axis...  35.3 us
    psum x1, blocking collectives, per_device(): squares = lax.psum(jnp.sum(summed * summed), 'slab')  12.3 us
    scatter-add x4, other arithmetic, per_device(): inject = jnp.zeros((block,), jnp.float32).at[rec_slot].add(misfits[level]...  9.37 us
    ppermute x7, starting transfers between devices, padded_2(): lax.ppermute(lax.slice_in_dim(block, 0, width, axis=dim), axis, backward)  9.01 us
    gather x4, local copies, waits for them, and re-layouts, record(): picked = field.reshape(-1)[rec_safe]  8.65 us
    ppermute x7, waiting for transfers between devices, padded_2(): lax.ppermute(lax.slice_in_dim(block, block.shape[dim] - width, None, axis...  4.85 us
    add x4, other arithmetic, per_device(): newer = 2.0 * current - older + scaled * accel + wavelet[level] * src_field  3.63 us
  transfers between devices with their start and end apart: 15, of which 8 were waited for; matrix products, arithmetic and copies ran while one was open for 14% of the time, Pallas kernels for 0%

commit v1 on v0

v1 whole, which is shorter than its diff:
```python
import functools

import jax
import jax.numpy as jnp
from jax import lax
from jax.experimental import pallas as pl
from jax.experimental.pallas import tpu as pltpu
from jax.sharding import PartitionSpec as P

STEPS = 4
MECH = 3
LINK = 2
PAD = 8
CHUNKS = 4
SUB = 24

center_coef = -2.5
near_coef = 4.0 / 3.0
far_coef = -1.0 / 12.0
courant = 0.14
relax_decay = (0.3, 0.7, 0.95)
relax_weight = (0.3, 0.2, 0.1)
update_rate = 0.05
tiny_eps = 1e-06

MESH = pl.DeviceIdType.MESH


def contract_lanes(a, b):
    return lax.dot_general(a, b, (((1,), (1,)), ((), ())), preferred_element_type=jnp.float32)


def kernel(
    shots,
    slabs,
    slowness_in,
    prev_in,
    now_in,
    memory_in,
    adj_now_in,
    adj_prev_in,
    wavelet,
    src_cells,
    src_signs,
    rec_cells,
    observed,
    total_out,
    inv_out,
    slow,
    older,
    field,
    relax,
    adj_now,
    adj_prev,
    drive,
    united,
    saved,
    back_relax,
    accum,
    scaled,
    factor,
    count,
    seen,
    source,
    pieces,
    halo,
    grad,
    parts,
    total,
    squares,
    load_sem,
    halo_send,
    halo_recv,
    part_send,
    part_recv,
    whole_send,
    whole_recv,
    square_send,
    square_recv,
):
    depth, width, lanes = slow.shape
    rows = width // CHUNKS
    stages = 2 * STEPS - 1
    me = lax.axis_index("slab")
    shot = lax.axis_index("shot")

    loads = [
        pltpu.make_async_copy(now_in.at[0], field.at[0, :, PAD : PAD + width], load_sem.at[0]),
        pltpu.make_async_copy(slowness_in, slow, load_sem.at[1]),
        pltpu.make_async_copy(memory_in.at[0], relax, load_sem.at[2]),
        pltpu.make_async_copy(prev_in.at[0], older, load_sem.at[3]),
        pltpu.make_async_copy(adj_now_in.at[0], adj_now, load_sem.at[4]),
        pltpu.make_async_copy(adj_prev_in.at[0], adj_prev, load_sem.at[5]),
    ]
    barrier = pltpu.get_barrier_semaphore()
    for k in range(1, slabs):
        pl.semaphore_signal(
            barrier, inc=1, device_id={"slab": lax.rem(me + k, slabs)}, device_id_type=MESH
        )
    for k in range(1, shots):
        pl.semaphore_signal(
            barrier, inc=1, device_id={"shot": lax.rem(shot + k, shots)}, device_id_type=MESH
        )
    for copy in loads:
        copy.start()
    pl.semaphore_wait(barrier, slabs - 1 + shots - 1)

    def outgoing(stage, side, c):
        first = depth - LINK if side == 0 else 0
        planes = pl.ds(first, LINK)
        start = pl.multiple_of(c * rows, 8)
        if stage == 0:
            src = now_in.at[0, planes, pl.ds(start, rows)]
        elif stage < STEPS:
            src = field.at[stage, planes, pl.ds(start + PAD, rows)]
        else:
            src = drive.at[stage - STEPS, planes, pl.ds(start + PAD, rows)]
        target = me + 1 if side == 0 else me - 1
        return pltpu.make_async_remote_copy(
            src_ref=src,
            dst_ref=halo.at[stage, side, :, pl.ds(start, rows)],
            send_sem=halo_send.at[stage, side, c],
            recv_sem=halo_recv.at[stage, side, c],
            device_id={"slab": target},
            device_id_type=MESH,
        )

    has_up = me < slabs - 1
    has_down = me > 0

    def send_halo(stage, c):
        @pl.when(has_up)
        def _():
            outgoing(stage, 0, c).start()

        @pl.when(has_down)
        def _():
            outgoing(stage, 1, c).start()

    def wait_sent(stage, c):
        @pl.when(has_up)
        def _():
            outgoing(stage, 0, c).wait_send()

        @pl.when(has_down)
        def _():
            outgoing(stage, 1, c).wait_send()

    def wait_halo(stage, c):
        @pl.when(has_down)
        def _():
            outgoing(stage, 0, c).wait_recv()

        @pl.when(has_up)
        def _():
            outgoing(stage, 1, c).wait_recv()

    for c in range(CHUNKS):
        send_halo(0, c)

    @pl.when(jnp.logical_not(has_down))
    def _():
        halo[:, 0] = jnp.zeros((stages, LINK, width, lanes), jnp.float32)

    @pl.when(jnp.logical_not(has_up))
    def _():
        halo[:, 1] = jnp.zeros((stages, LINK, width, lanes), jnp.float32)

    edge = jnp.zeros((depth, PAD, lanes), jnp.float32)
    for n in range(STEPS):
        field[n, :, :PAD] = edge
        field[n, :, PAD + width :] = edge
    for n in range(STEPS - 1):
        drive[n, :, :PAD] = edge
        drive[n, :, PAD + width :] = edge

    def one_hot(index, height):
        at = lax.broadcasted_iota(jnp.int32, (height, index.shape[1]), 0)
        return jnp.where(at == index, 1.0, 0.0)

    first_row = me * (depth * width)
    rec = rec_cells[...]
    rec_row = lax.div(rec, lanes)
    rec_lane = rec - rec_row * lanes
    rec_row = rec_row - first_row
    at_lane = one_hot(rec_lane, lanes)
    pieces[0:lanes] = at_lane.astype(jnp.bfloat16)
    for n in range(STEPS):
        rest = at_lane * observed[0, n : n + 1, :]
        for k in range(3):
            part = rest.astype(jnp.bfloat16)
            begin = (1 + 3 * n + k) * lanes
            pieces[begin : begin + lanes] = part
            rest = rest - part.astype(jnp.float32)
    src = src_cells[...]
    src_row = lax.div(src, lanes)
    src_lane = src - src_row * lanes
    src_row = src_row - first_row
    src_at = (one_hot(src_lane, lanes) * src_signs[...].astype(jnp.float32)).astype(jnp.bfloat16)
    for d in range(depth):
        at_row = one_hot(rec_row - d * width, width).astype(jnp.bfloat16)
        count[d] = contract_lanes(at_row, pieces[0:lanes])
        for n in range(STEPS):
            begin = (1 + 3 * n) * lanes
            got = contract_lanes(at_row, pieces[begin : begin + 3 * lanes])
            seen[n, d] = (
                got[:, 2 * lanes :] + got[:, lanes : 2 * lanes]
            ) + got[:, :lanes]
        src_rows = one_hot(src_row - d * width, width).astype(jnp.bfloat16)
        source[d] = contract_lanes(src_rows, src_at)

    loads[1].wait()
    for d in range(depth):
        s = slow[d]
        held = courant / (s * s)
        scaled[d] = held
        factor[d] = (-2.0 * held) / s
    for k in (0, 2, 3, 4, 5):
        loads[k].wait()

    lane = lax.broadcasted_iota(jnp.int32, (8, lanes), 1)[:1]
    left_1 = jnp.where(lane >= 1, near_coef, 0.0)
    left_2 = jnp.where(lane >= 2, far_coef, 0.0)
    right_1 = jnp.where(lane < lanes - 1, near_coef, 0.0)
    right_2 = jnp.where(lane < lanes - 2, far_coef, 0.0)

    def laplace(ref, n, stage, d, r):
        def plane(q):
            if q < 0:
                return halo[stage, 0, q + LINK, pl.ds(r, SUB)]
            if q >= depth:
                return halo[stage, 1, q - depth, pl.ds(r, SUB)]
            return ref[n, q, pl.ds(r + PAD, SUB)]

        mid = ref[n, d, pl.ds(r + PAD, SUB)]
        near = (plane(d - 1) + plane(d + 1)) + (
            ref[n, d, pl.ds(r + PAD - 1, SUB)] + ref[n, d, pl.ds(r + PAD + 1, SUB)]
        )
        far = (plane(d - 2) + plane(d + 2)) + (
            ref[n, d, pl.ds(r + PAD - 2, SUB)] + ref[n, d, pl.ds(r + PAD + 2, SUB)]
        )
        along = (
            left_1 * pltpu.roll(mid, 1, 1)
            + right_1 * pltpu.roll(mid, lanes - 1, 1)
            + left_2 * pltpu.roll(mid, 2, 1)
            + right_2 * pltpu.roll(mid, lanes - 2, 1)
        )
        return (3.0 * center_coef) * mid + near_coef * near + far_coef * far + along, mid

    def blocks(c, body):
        for d in range(depth):
            for k in range(rows // SUB):
                body(d, pl.multiple_of(c * rows + k * SUB, 8))

    def adjoint_part(level, d, r, back, begin_accum):
        at = pl.ds(r, SUB)
        up = back + (
            count[d, at] * field[level + 1, d, pl.ds(r + PAD, SUB)] - seen[level, d, at]
        )
        term = up * saved[level, d, at]
        term = term if begin_accum else accum[d, at] + term
        if level == 0:
            grad[d, at] = term * factor[d, at]
            return
        accum[d, at] = term
        united[level, d, at] = up
        pushed = scaled[d, at] * up
        out = pushed
        for m in range(MECH):
            if begin_accum:
                back_relax[m, d, at] = pushed
            else:
                held = back_relax[m, d, at]
                out = out - relax_weight[m] * held
                if level > 1:
                    back_relax[m, d, at] = relax_decay[m] * held + pushed
        drive[STEPS - 1 - level, d, pl.ds(r + PAD, SUB)] = out

    def forward_stage(n):
        amount = wavelet[n]

        def chunk(c, carry):
            wait_halo(n, c)
            if n > 0:
                wait_sent(n - 1, c)

            def body(d, r):
                at = pl.ds(r, SUB)
                inner = pl.ds(r + PAD, SUB)
                curved, mid = laplace(field, n, n, d, r)
                held = [relax[m, d, at] for m in range(MECH)]
                accel = curved + ((held[0] + held[1]) + held[2])
                before = older[d, at] if n == 0 else field[n - 1, d, inner]
                saved[n, d, at] = accel
                field[n + 1, d, inner] = (
                    (2.0 * mid - before) + scaled[d, at] * accel + amount * source[d, at]
                )
                if n < STEPS - 1:
                    for m in range(MECH):
                        relax[m, d, at] = relax_decay[m] * held[m] - relax_weight[m] * curved
                else:
                    adjoint_part(STEPS - 1, d, r, adj_now[d, at], True)

            blocks(c, body)
            send_halo(n + 1, c)
            return carry

        lax.fori_loop(0, CHUNKS, chunk, 0)

    piece = depth * rows // shots

    def spot(owner, c):
        begin = owner * piece
        return begin // rows, pl.multiple_of(c * rows + begin % rows, 8)

    def part_copy(k, c):
        target = lax.rem(shot + k, shots)
        d, r = spot(target, c)
        return pltpu.make_async_remote_copy(
            src_ref=grad.at[d, pl.ds(r, piece)],
            dst_ref=parts.at[c, k - 1],
            send_sem=part_send.at[c, k - 1],
            recv_sem=part_recv.at[c, k - 1],
            device_id={"shot": target},
            device_id_type=MESH,
        )

    def whole_copy(k, c):
        target = lax.rem(shot + k, shots)
        d, r = spot(shot, c)
        return pltpu.make_async_remote_copy(
            src_ref=total.at[d, pl.ds(r, piece)],
            dst_ref=total.at[d, pl.ds(r, piece)],
            send_sem=whole_send.at[c, k - 1],
            recv_sem=whole_recv.at[c, k - 1],
            device_id={"shot": target},
            device_id_type=MESH,
        )

    def reduce_chunk(c):
        d, r = spot(shot, c)
        held = grad[d, pl.ds(r, piece)]
        for k in range(1, shots):
            part_copy(k, c).wait_recv()
            held = held + parts[c, k - 1]
        total[d, pl.ds(r, piece)] = held
        for k in range(1, shots):
            whole_copy(k, c).start()

    def backward_stage(level):
        stage = 2 * STEPS - 2 - level

        def chunk(c, carry):
            wait_halo(stage, c)
            wait_sent(stage - 1, c)

            def body(d, r):
                at = pl.ds(r, SUB)
                curved, _ = laplace(drive, stage - STEPS, stage, d, r)
                after = united[level + 1, d, at]
                if level == STEPS - 2:
                    base = adj_prev[d, at]
                else:
                    base = -united[level + 2, d, at]
                adjoint_part(level, d, r, (base + 2.0 * after) + curved, False)

            blocks(c, body)
            if level > 0:
                send_halo(stage + 1, c)
            else:
                for k in range(1, shots):
                    part_copy(k, c).start()

                @pl.when(c >= 2)
                def _():
                    reduce_chunk(c - 2)

            return carry

        lax.fori_loop(0, CHUNKS, chunk, 0)

    for n in range(STEPS):
        forward_stage(n)
    for level in reversed(range(STEPS - 1)):
        backward_stage(level)
    for c in range(CHUNKS - 2, CHUNKS):
        reduce_chunk(c)

    def settle(c, carry):
        wait_sent(stages - 1, c)
        for k in range(1, shots):
            part_copy(k, c).wait_send()
            whole_copy(k, c).wait()
        return carry

    lax.fori_loop(0, CHUNKS, settle, 0)

    store = pltpu.make_async_copy(total, total_out, load_sem.at[0])
    store.start()

    summed = jnp.zeros((8, lanes), jnp.float32)
    for d in range(depth):
        block = total[d]
        summed = summed + jnp.sum((block * block).reshape(width // 8, 8, lanes), axis=0)
    squares[me] = summed

    def square_copy(k):
        return pltpu.make_async_remote_copy(
            src_ref=squares.at[me],
            dst_ref=squares.at[me],
            send_sem=square_send.at[k - 1],
            recv_sem=square_recv.at[k - 1],
            device_id={"slab": lax.rem(me + k, slabs)},
            device_id_type=MESH,
        )

    for k in range(1, slabs):
        square_copy(k).start()
    for k in range(1, slabs):
        square_copy(k).wait()
    everything = squares[0]
    for k in range(1, slabs):
        everything = everything + squares[k]
    cells = slabs * depth * width * lanes
    mean = jnp.sum(everything, keepdims=True) / cells + tiny_eps
    inv_out[...] = jnp.broadcast_to(1.0 / jnp.sqrt(mean), inv_out.shape)
    store.wait()


def per_device(
    slowness,
    wave_prev,
    wave_now,
    memory,
    adjoint_now,
    adjoint_prev,
    wavelet,
    src_cells,
    src_signs,
    rec_cells,
    observed,
):
    depth, width, lanes = slowness.shape
    shots, slabs = lax.axis_size("shot"), lax.axis_size("slab")
    rows = width // CHUNKS
    piece = depth * rows // shots
    assert width % CHUNKS == 0 and rows % SUB == 0 and depth >= LINK
    assert depth * rows % shots == 0 and rows % piece == 0 and piece % 8 == 0
    receivers = rec_cells.shape[0]
    stages = 2 * STEPS - 1
    f32 = jnp.float32
    block = (depth, width, lanes)
    padded = (depth, width + 2 * PAD, lanes)
    anywhere = pl.BlockSpec(memory_space=pl.ANY)
    vmem = pl.BlockSpec(memory_space=pltpu.VMEM)
    smem = pl.BlockSpec(memory_space=pltpu.SMEM)
    dma = pltpu.SemaphoreType.DMA
    total, inverse = pl.pallas_call(
        functools.partial(kernel, shots, slabs),
        name="invert",
        out_shape=(
            jax.ShapeDtypeStruct(block, f32),
            jax.ShapeDtypeStruct((8, lanes), f32),
        ),
        in_specs=[anywhere] * 6 + [smem] + [vmem] * 4,
        out_specs=(anywhere, vmem),
        scratch_shapes=[
            pltpu.VMEM(block, f32),
            pltpu.VMEM(block, f32),
            pltpu.VMEM((STEPS + 1, *padded), f32),
            pltpu.VMEM((MECH, *block), f32),
            pltpu.VMEM(block, f32),
            pltpu.VMEM(block, f32),
            pltpu.VMEM((STEPS - 1, *padded), f32),
            pltpu.VMEM((STEPS, *block), f32),
            pltpu.VMEM((STEPS, *block), f32),
            pltpu.VMEM((MECH, *block), f32),
            pltpu.VMEM(block, f32),
            pltpu.VMEM(block, f32),
            pltpu.VMEM(block, f32),
            pltpu.VMEM(block, f32),
            pltpu.VMEM((STEPS, *block), f32),
            pltpu.VMEM(block, f32),
            pltpu.VMEM(((1 + 3 * STEPS) * lanes, receivers), jnp.bfloat16),
            pltpu.VMEM((stages, 2, LINK, width, lanes), f32),
            pltpu.VMEM(block, f32),
            pltpu.VMEM((CHUNKS, shots - 1, piece, lanes), f32),
            pltpu.VMEM(block, f32),
            pltpu.VMEM((slabs, 8, lanes), f32),
            dma((6,)),
            dma((stages, 2, CHUNKS)),
            dma((stages, 2, CHUNKS)),
            dma((CHUNKS, shots - 1)),
            dma((CHUNKS, shots - 1)),
            dma((CHUNKS, shots - 1)),
            dma((CHUNKS, shots - 1)),
            dma((slabs - 1,)),
            dma((slabs - 1,)),
        ],
        compiler_params=pltpu.CompilerParams(
            collective_id=0, has_side_effects=True, vmem_limit_bytes=40 * 2**20
        ),
    )(
        slowness,
        wave_prev,
        wave_now,
        memory,
        adjoint_now,
        adjoint_prev,
        wavelet,
        src_cells,
        src_signs,
        rec_cells.reshape(1, receivers),
        observed,
    )
    normed = total * inverse[0, 0]
    new_slowness = slowness - update_rate * normed
    share = width // shots
    gradient = lax.dynamic_slice_in_dim(normed, lax.axis_index("shot") * share, share, 1)
    return (new_slowness, gradient)


def solution(mesh):
    in_specs = (
        P(("groups", "slab"), None, None),
        P(("groups", "shot"), "slab", None, None),
        P(("groups", "shot"), "slab", None, None),
        P(("groups", "shot"), None, "slab", None, None),
        P(("groups", "shot"), "slab", None, None),
        P(("groups", "shot"), "slab", None, None),
        P(),
        P(("groups", "shot"), None),
        P(("groups", "shot"), None),
        P("groups"),
        P(("groups", "shot"), None, None),
    )
    out_specs = (P(("groups", "slab"), None, None), P(("groups", "slab"), "shot", None))
    return jax.shard_map(
        per_device, mesh=mesh, in_specs=in_specs, out_specs=out_specs, check_vma=False
    )
```

time: 168 us -> 63 us (0.38)
  Pallas kernels: 0 us -> 49.8 us
  waiting for transfers between devices: 44.7 us -> 0 us
  starting transfers between devices: 44.4 us -> 0 us
  other arithmetic: 33.3 us -> 1.44 us
  between operations: 15.2 us -> 0.66 us
  blocking collectives: 12.3 us -> 0 us
  local copies, waits for them, and re-layouts: 17 us -> 10.7 us
    pallas_call x0 -> x1, Pallas kernels: none -> 49.8 us  [per_device(): pl.pallas_call(functools.partial(kernel, shots, slabs), name='invert', ou...]
    ppermute x14 -> x0, starting transfers between devices: 44.4 us -> none  [the longest x7 35.3 us: padded_2(): lax.ppermute(lax.slice_in_dim(block, block.shape[dim] - width, None, axis...]
    psum x1 -> x0, waiting for transfers between devices: 36.6 us -> none  [per_device(): summed = lax.psum(local_grad, 'shot')]
    psum x1 -> x0, blocking collectives: 12.3 us -> none  [per_device(): squares = lax.psum(jnp.sum(summed * summed), 'slab')]
    scatter-add x5 -> x0, other arithmetic: 10.4 us -> none  [the longest x4 9.37 us: per_device(): inject = jnp.zeros((block,), jnp.float32).at[rec_slot].add(misfits[level]...]
    gather x4 -> x0, local copies, waits for them, and re-layouts: 8.65 us -> none  [record(): picked = field.reshape(-1)[rec_safe]]
    ppermute x14 -> x0, waiting for transfers between devices: 8.05 us -> none  [the longest x7 4.85 us: padded_2(): lax.ppermute(lax.slice_in_dim(block, block.shape[dim] - width, None, axis...]
    unnamed x34 -> x22, local copies, waits for them, and re-layouts: 2.17 us -> 9.57 us
  transfers between devices with their start and end apart: 15 -> 0, of which waited for: 8 -> 0; matrix products, arithmetic and copies ran while one was open for 14% -> 0% of each run, Pallas kernels for 0% -> 0%
where the time goes in v1:
time: 63 us; the launch traced here: 62.6 us
  Pallas kernels  49.8 us (79%)
  local copies, waits for them, and re-layouts  10.7 us (17%)
  other arithmetic  1.44 us (2%)
  between operations  0.66 us (1%)
    pallas_call x1, Pallas kernels, per_device(): pl.pallas_call(functools.partial(kernel, shots, slabs), name='invert', ou...  49.8 us
    unnamed x22, local copies, waits for them, and re-layouts  9.57 us
    sub x1, other arithmetic, per_device(): new_slowness = slowness - update_rate * normed  1.44 us

profile of v1, /device:TPU:0, one launch (start us, length us, event | category | flops | bytes accessed | tf_op | source)
XLA Modules:
  0.0 62.6 jit_solution(13585612081535134087)
XLA Ops:
  0.6 0.0 copy-start
  0.6 1.0 %copy-done = f32[4,192,128]{2,1,0:T(8,128)S(1)} copy-done((f32[4,192,128]{2,1,0:T(8,128)S(1)}, f32[4,192,128]{2,1,0:T(8,128)}, u32[]{:S(2)}) %copy-start) | copy-done | bytes 393240
  1.6 0.0 copy-start.1
  1.6 1.3 %copy-done.1 = f32[1,3,4,192,128]{4,3,2,1,0:T(8,128)S(1)} copy-done((f32[1,3,4,192,128]{4,3,2,1,0:T(8,128)S(1)}, f32[1,3,4,192,128]{4,3,2,1,0:T(8,128)}, u32[]{:S(2)}) %copy-start.1) | copy-done | bytes 1179672
  2.9 0.0 copy-start.2
  2.9 1.0 %copy-done.2 = f32[1,4,192,128]{3,2,1,0:T(8,128)S(1)} copy-done((f32[1,4,192,128]{3,2,1,0:T(8,128)S(1)}, f32[1,4,192,128]{3,2,1,0:T(8,128)}, u32[]{:S(2)}) %copy-start.2) | copy-done | bytes 393240
  3.9 0.0 copy-start.3
  3.9 1.0 %copy-done.3 = f32[1,4,192,128]{3,2,1,0:T(8,128)S(1)} copy-done((f32[1,4,192,128]{3,2,1,0:T(8,128)S(1)}, f32[1,4,192,128]{3,2,1,0:T(8,128)}, u32[]{:S(2)}) %copy-start.3) | copy-done | bytes 393240
  4.9 0.0 copy-start.4
  4.9 1.0 %copy-done.4 = f32[1,4,192,128]{3,2,1,0:T(8,128)S(1)} copy-done((f32[1,4,192,128]{3,2,1,0:T(8,128)S(1)}, f32[1,4,192,128]{3,2,1,0:T(8,128)}, u32[]{:S(2)}) %copy-start.4) | copy-done | bytes 393240
  5.9 0.0 copy-start.5
  5.9 1.0 %copy-done.5 = f32[1,4,192,128]{3,2,1,0:T(8,128)S(1)} copy-done((f32[1,4,192,128]{3,2,1,0:T(8,128)S(1)}, f32[1,4,192,128]{3,2,1,0:T(8,128)}, u32[]{:S(2)}) %copy-start.5) | copy-done | bytes 393240
  6.9 0.0 copy-start.6
  6.9 0.7 %copy-done.6 = f32[1,4,256]{2,1,0:T(4,128)S(1)} copy-done((f32[1,4,256]{2,1,0:T(4,128)S(1)}, f32[1,4,256]{2,1,0:T(4,128)}, u32[]{:S(2)}) %copy-start.6) | copy-done | bytes 4120
  7.6 0.0 copy-start.7
  7.6 0.7 %copy-done.7 = s32[256]{0:T(256)S(1)} copy-done((s32[256]{0:T(256)S(1)}, s32[256]{0:T(256)}, u32[]{:S(2)}) %copy-start.7) | copy-done | bytes 1048
  8.3 0.0 copy-start.8
  8.3 0.7 %copy-done.8 = f32[4]{0:T(128)S(1)} copy-done((f32[4]{0:T(128)S(1)}, f32[4]{0:T(128)}, u32[]{:S(2)}) %copy-start.8) | copy-done | bytes 40
  8.9 0.7 %copy-done.9 = s32[1,64]{1,0:T(1,128)S(1)} copy-done((s32[1,64]{1,0:T(1,128)S(1)}, s32[1,64]{1,0:T(1,128)}, u32[]{:S(2)}) %copy-start.9) | copy-done | bytes 280
  9.6 0.7 %copy-done.10 = s32[1,64]{1,0:T(1,128)S(1)} copy-done((s32[1,64]{1,0:T(1,128)S(1)}, s32[1,64]{1,0:T(1,128)}, u32[]{:S(2)}) %copy-start.10) | copy-done | bytes 280
  10.2 49.8 %invert.1 = (f32[4,192,128]{2,1,0:T(8,128)S(1)}, f32[8,128]{1,0:T(8,128)S(1)}) custom-call(f32[4,192,128]{2,1,0:T(8,128)S(1)} %copy-done, f32[1,4,192,128]{3,2,1,0:T(8,128)S(1)} %copy-done.2, f32[1,4,192,128]{3,2,1,0:T(8,128)S(1)} %copy-done.3, f32[1,3,4,192,128]{4,3,2,1,0:T(8,128)S(1)} %copy-done.1, f32[1,4,192,128]{3,2,1,0:T(8,128)S(1)} %copy-done.4, ...), custom_call_target="tpu_custom_call" | custom-call | tf_op jit(solution)/shard_map/invert/pallas_call | solution.py:458
  60.0 0.5 slice.3
  60.5 1.4 %multiply_subtract_fusion = (f32[4,192,128]{2,1,0:T(8,128)}, f32[4,192,128]{2,1,0:T(8,128)S(1)}) fusion(f32[4,192,128]{2,1,0:T(8,128)S(1)} %copy-done, f32[4,192,128]{2,1,0:T(8,128)S(1)} %get-tuple-element.4, f32[]{:T(128)} %bitcast.1), kind=kLoop, calls=%fused_computation | loop fusion | flops 294912 | bytes 1572868 | tf_op jit(solution)/shard_map/sub | solution.py:517
  62.0 0.6 %constant_dynamic-slice_fusion = f32[4,48,128]{2,1,0:T(8,128)} fusion(f32[4,192,128]{2,1,0:T(8,128)S(1)} %get-tuple-element.7, s32[]{:T(128)S(6)} %select_n.3), kind=kLoop, calls=%fused_computation.2 | loop fusion | bytes 196612 | tf_op jit(solution)/shard_map/dynamic_slice | solution.py:519
  (2 shorter events, 0.0 us)
Async XLA Ops:
  0.6 1.0 %copy-start = (f32[4,192,128]{2,1,0:T(8,128)S(1)}, f32[4,192,128]{2,1,0:T(8,128)}, u32[]{:S(2)}) copy-start(f32[4,192,128]{2,1,0:T(8,128)} %slowness_in.1) | copy-start | bytes 1179652
  1.6 1.3 %copy-start.1 = (f32[1,3,4,192,128]{4,3,2,1,0:T(8,128)S(1)}, f32[1,3,4,192,128]{4,3,2,1,0:T(8,128)}, u32[]{:S(2)}) copy-start(f32[1,3,4,192,128]{4,3,2,1,0:T(8,128)} %memory_in.1) | copy-start | bytes 3538948
  2.9 1.0 %copy-start.2 = (f32[1,4,192,128]{3,2,1,0:T(8,128)S(1)}, f32[1,4,192,128]{3,2,1,0:T(8,128)}, u32[]{:S(2)}) copy-start(f32[1,4,192,128]{3,2,1,0:T(8,128)} %prev_in.1) | copy-start | bytes 1179652
  3.9 1.0 %copy-start.3 = (f32[1,4,192,128]{3,2,1,0:T(8,128)S(1)}, f32[1,4,192,128]{3,2,1,0:T(8,128)}, u32[]{:S(2)}) copy-start(f32[1,4,192,128]{3,2,1,0:T(8,128)} %now_in.1) | copy-start | bytes 1179652
  4.9 1.0 %copy-start.4 = (f32[1,4,192,128]{3,2,1,0:T(8,128)S(1)}, f32[1,4,192,128]{3,2,1,0:T(8,128)}, u32[]{:S(2)}) copy-start(f32[1,4,192,128]{3,2,1,0:T(8,128)} %adj_now_in.1) | copy-start | bytes 1179652
  5.9 1.0 %copy-start.5 = (f32[1,4,192,128]{3,2,1,0:T(8,128)S(1)}, f32[1,4,192,128]{3,2,1,0:T(8,128)}, u32[]{:S(2)}) copy-start(f32[1,4,192,128]{3,2,1,0:T(8,128)} %adj_prev_in.1) | copy-start | bytes 1179652
  6.9 0.7 %copy-start.6 = (f32[1,4,256]{2,1,0:T(4,128)S(1)}, f32[1,4,256]{2,1,0:T(4,128)}, u32[]{:S(2)}) copy-start(f32[1,4,256]{2,1,0:T(4,128)} %observed.1) | copy-start | bytes 12292
  7.6 0.7 %copy-start.7 = (s32[256]{0:T(256)S(1)}, s32[256]{0:T(256)}, u32[]{:S(2)}) copy-start(s32[256]{0:T(256)} %param.20) | copy-start | bytes 3076
  8.3 0.7 %copy-start.8 = (f32[4]{0:T(128)S(1)}, f32[4]{0:T(128)}, u32[]{:S(2)}) copy-start(f32[4]{0:T(128)} %wavelet.1) | copy-start | bytes 52
  8.9 0.7 %copy-start.9 = (s32[1,64]{1,0:T(1,128)S(1)}, s32[1,64]{1,0:T(1,128)}, u32[]{:S(2)}) copy-start(s32[1,64]{1,0:T(1,128)} %src_cells.1) | copy-start | bytes 772
  9.6 0.7 %copy-start.10 = (s32[1,64]{1,0:T(1,128)S(1)}, s32[1,64]{1,0:T(1,128)}, u32[]{:S(2)}) copy-start(s32[1,64]{1,0:T(1,128)} %src_signs.1) | copy-start | bytes 772

commit v2 on v1

--- a/solution.py
+++ b/solution.py
@@ -62,6 +62,7 @@
     count,
     seen,
     source,
+    hot_rows,
     pieces,
     halo,
     grad,
@@ -179,35 +180,34 @@
         return jnp.where(at == index, 1.0, 0.0)
 
     first_row = me * (depth * width)
-    rec = rec_cells[...]
-    rec_row = lax.div(rec, lanes)
-    rec_lane = rec - rec_row * lanes
-    rec_row = rec_row - first_row
-    at_lane = one_hot(rec_lane, lanes)
-    pieces[0:lanes] = at_lane.astype(jnp.bfloat16)
-    for n in range(STEPS):
-        rest = at_lane * observed[0, n : n + 1, :]
-        for k in range(3):
-            part = rest.astype(jnp.bfloat16)
-            begin = (1 + 3 * n + k) * lanes
-            pieces[begin : begin + lanes] = part
-            rest = rest - part.astype(jnp.float32)
     src = src_cells[...]
     src_row = lax.div(src, lanes)
     src_lane = src - src_row * lanes
-    src_row = src_row - first_row
     src_at = (one_hot(src_lane, lanes) * src_signs[...].astype(jnp.float32)).astype(jnp.bfloat16)
-    for d in range(depth):
-        at_row = one_hot(rec_row - d * width, width).astype(jnp.bfloat16)
-        count[d] = contract_lanes(at_row, pieces[0:lanes])
+    src_rows = one_hot(src_row - first_row, depth * width).astype(jnp.bfloat16)
+    source[...] = contract_lanes(src_rows, src_at).reshape(depth, width, lanes)
+
+    def place_receivers():
+        rec = rec_cells[...]
+        rec_row = lax.div(rec, lanes)
+        rec_lane = rec - rec_row * lanes
+        at_lane = one_hot(rec_lane, lanes)
+        pieces[0:lanes] = at_lane.astype(jnp.bfloat16)
         for n in range(STEPS):
-            begin = (1 + 3 * n) * lanes
-            got = contract_lanes(at_row, pieces[begin : begin + 3 * lanes])
-            seen[n, d] = (
-                got[:, 2 * lanes :] + got[:, lanes : 2 * lanes]
-            ) + got[:, :lanes]
-        src_rows = one_hot(src_row - d * width, width).astype(jnp.bfloat16)
-        source[d] = contract_lanes(src_rows, src_at)
+            rest = at_lane * observed[0, n : n + 1, :]
+            for k in range(3):
+                part = rest.astype(jnp.bfloat16)
+                begin = (1 + 3 * n + k) * lanes
+                pieces[begin : begin + lanes] = part
+                rest = rest - part.astype(jnp.float32)
+        hot_rows[...] = one_hot(rec_row - first_row, depth * width).astype(jnp.bfloat16)
+        count[...] = contract_lanes(hot_rows[...], pieces[0:lanes]).reshape(depth, width, lanes)
+
+    def place_observed(n):
+        begin = (1 + 3 * n) * lanes
+        got = contract_lanes(hot_rows[...], pieces[begin : begin + 3 * lanes])
+        got = (got[:, 2 * lanes :] + got[:, lanes : 2 * lanes]) + got[:, :lanes]
+        seen[n] = got.reshape(depth, width, lanes)
 
     loads[1].wait()
     for d in range(depth):
@@ -224,33 +224,33 @@
     right_1 = jnp.where(lane < lanes - 1, near_coef, 0.0)
     right_2 = jnp.where(lane < lanes - 2, far_coef, 0.0)
 
-    def laplace(ref, n, stage, d, r):
-        def plane(q):
-            if q < 0:
-                return halo[stage, 0, q + LINK, pl.ds(r, SUB)]
-            if q >= depth:
-                return halo[stage, 1, q - depth, pl.ds(r, SUB)]
-            return ref[n, q, pl.ds(r + PAD, SUB)]
-
-        mid = ref[n, d, pl.ds(r + PAD, SUB)]
-        near = (plane(d - 1) + plane(d + 1)) + (
-            ref[n, d, pl.ds(r + PAD - 1, SUB)] + ref[n, d, pl.ds(r + PAD + 1, SUB)]
-        )
-        far = (plane(d - 2) + plane(d + 2)) + (
-            ref[n, d, pl.ds(r + PAD - 2, SUB)] + ref[n, d, pl.ds(r + PAD + 2, SUB)]
-        )
-        along = (
-            left_1 * pltpu.roll(mid, 1, 1)
-            + right_1 * pltpu.roll(mid, lanes - 1, 1)
-            + left_2 * pltpu.roll(mid, 2, 1)
-            + right_2 * pltpu.roll(mid, lanes - 2, 1)
-        )
-        return (3.0 * center_coef) * mid + near_coef * near + far_coef * far + along, mid
+    def laplace(ref, n, stage, r):
+        def rows_at(d, shift):
+            return ref[n, d, pl.ds(r + PAD + shift, SUB)]
+
+        low = [halo[stage, 0, k, pl.ds(r, SUB)] for k in range(LINK)]
+        mids = [rows_at(d, 0) for d in range(depth)]
+        high = [halo[stage, 1, k, pl.ds(r, SUB)] for k in range(LINK)]
+        planes = low + mids + high
+        curved = []
+        for d in range(depth):
+            mid = mids[d]
+            near = (planes[d + 1] + planes[d + 3]) + (rows_at(d, -1) + rows_at(d, 1))
+            far = (planes[d] + planes[d + 4]) + (rows_at(d, -2) + rows_at(d, 2))
+            along = (
+                left_1 * pltpu.roll(mid, 1, 1)
+                + right_1 * pltpu.roll(mid, lanes - 1, 1)
+                + left_2 * pltpu.roll(mid, 2, 1)
+                + right_2 * pltpu.roll(mid, lanes - 2, 1)
+            )
+            curved.append(
+                (3.0 * center_coef) * mid + near_coef * near + far_coef * far + along
+            )
+        return curved, mids
 
     def blocks(c, body):
-        for d in range(depth):
-            for k in range(rows // SUB):
-                body(d, pl.multiple_of(c * rows + k * SUB, 8))
+        for k in range(rows // SUB):
+            body(pl.multiple_of(c * rows + k * SUB, 8))
 
     def adjoint_part(level, d, r, back, begin_accum):
         at = pl.ds(r, SUB)
@@ -284,22 +284,25 @@
             if n > 0:
                 wait_sent(n - 1, c)
 
-            def body(d, r):
+            def body(r):
                 at = pl.ds(r, SUB)
                 inner = pl.ds(r + PAD, SUB)
-                curved, mid = laplace(field, n, n, d, r)
-                held = [relax[m, d, at] for m in range(MECH)]
-                accel = curved + ((held[0] + held[1]) + held[2])
-                before = older[d, at] if n == 0 else field[n - 1, d, inner]
-                saved[n, d, at] = accel
-                field[n + 1, d, inner] = (
-                    (2.0 * mid - before) + scaled[d, at] * accel + amount * source[d, at]
-                )
-                if n < STEPS - 1:
-                    for m in range(MECH):
-                        relax[m, d, at] = relax_decay[m] * held[m] - relax_weight[m] * curved
-                else:
-                    adjoint_part(STEPS - 1, d, r, adj_now[d, at], True)
+                curved, mids = laplace(field, n, n, r)
+                for d in range(depth):
+                    held = [relax[m, d, at] for m in range(MECH)]
+                    accel = curved[d] + ((held[0] + held[1]) + held[2])
+                    before = older[d, at] if n == 0 else field[n - 1, d, inner]
+                    newer = (2.0 * mids[d] - before) + scaled[d, at] * accel
+                    newer = newer + amount * source[d, at]
+                    saved[n, d, at] = accel
+                    field[n + 1, d, inner] = newer
+                    if n < STEPS - 1:
+                        for m in range(MECH):
+                            relax[m, d, at] = (
+                                relax_decay[m] * held[m] - relax_weight[m] * curved[d]
+                            )
+                    else:
+                        adjoint_part(n, d, r, adj_now[d, at], True)
 
             blocks(c, body)
             send_halo(n + 1, c)
@@ -354,15 +357,16 @@
             wait_halo(stage, c)
             wait_sent(stage - 1, c)
 
-            def body(d, r):
+            def body(r):
                 at = pl.ds(r, SUB)
-                curved, _ = laplace(drive, stage - STEPS, stage, d, r)
-                after = united[level + 1, d, at]
-                if level == STEPS - 2:
-                    base = adj_prev[d, at]
-                else:
-                    base = -united[level + 2, d, at]
-                adjoint_part(level, d, r, (base + 2.0 * after) + curved, False)
+                curved, _ = laplace(drive, stage - STEPS, stage, r)
+                for d in range(depth):
+                    after = united[level + 1, d, at]
+                    if level == STEPS - 2:
+                        base = adj_prev[d, at]
+                    else:
+                        base = -united[level + 2, d, at]
+                    adjoint_part(level, d, r, (base + 2.0 * after) + curved[d], False)
 
             blocks(c, body)
             if level > 0:
@@ -381,6 +385,11 @@
 
     for n in range(STEPS):
         forward_stage(n)
+        if n == 0:
+            place_receivers()
+        if n in (1, 2):
+            for k in (2 * n - 2, 2 * n - 1):
+                place_observed(k)
     for level in reversed(range(STEPS - 1)):
         backward_stage(level)
     for c in range(CHUNKS - 2, CHUNKS):
@@ -425,6 +434,15 @@
     mean = jnp.sum(everything, keepdims=True) / cells + tiny_eps
     inv_out[...] = jnp.broadcast_to(1.0 / jnp.sqrt(mean), inv_out.shape)
     store.wait()
+
+
+def finish(total, slowness, inverse, new_slowness, gradient):
+    share = gradient.shape[1]
+    first = pl.multiple_of(lax.axis_index("shot") * share, 8)
+    inv = inverse[0:1]
+    for d in range(total.shape[0]):
+        new_slowness[d] = slowness[d] - update_rate * (total[d] * inv)
+        gradient[d] = total[d, pl.ds(first, share)] * inv
 
 
 def per_device(
@@ -481,6 +499,7 @@
             pltpu.VMEM(block, f32),
             pltpu.VMEM((STEPS, *block), f32),
             pltpu.VMEM(block, f32),
+            pltpu.VMEM((depth * width, receivers), jnp.bfloat16),
             pltpu.VMEM(((1 + 3 * STEPS) * lanes, receivers), jnp.bfloat16),
             pltpu.VMEM((stages, 2, LINK, width, lanes), f32),
             pltpu.VMEM(block, f32),
@@ -498,7 +517,7 @@
             dma((slabs - 1,)),
         ],
         compiler_params=pltpu.CompilerParams(
-            collective_id=0, has_side_effects=True, vmem_limit_bytes=40 * 2**20
+            collective_id=0, has_side_effects=True, vmem_limit_bytes=60 * 2**20
         ),
     )(
         slowness,
@@ -513,10 +532,18 @@
         rec_cells.reshape(1, receivers),
         observed,
     )
-    normed = total * inverse[0, 0]
-    new_slowness = slowness - update_rate * normed
     share = width // shots
-    gradient = lax.dynamic_slice_in_dim(normed, lax.axis_index("shot") * share, share, 1)
+    new_slowness, gradient = pl.pallas_call(
+        finish,
+        name="finish",
+        out_shape=(
+            jax.ShapeDtypeStruct(block, f32),
+            jax.ShapeDtypeStruct((depth, share, lanes), f32),
+        ),
+        in_specs=[vmem] * 3,
+        out_specs=(vmem, vmem),
+        compiler_params=pltpu.CompilerParams(vmem_limit_bytes=60 * 2**20),
+    )(total, slowness, inverse)
     return (new_slowness, gradient)
 
 

time: 63 us -> 53.4 us (0.85)
  local copies, waits for them, and re-layouts: 10.7 us -> 0 us
  Pallas kernels: 49.8 us -> 52.6 us
  other arithmetic: 1.44 us -> 0 us
    unnamed x22 -> x0, local copies, waits for them, and re-layouts: 9.57 us -> none
    pallas_call x0 -> x1, Pallas kernels: none -> 1.95 us  [per_device(): pl.pallas_call(finish, name='finish', out_shape=(jax.ShapeDtypeStruct(blo...]
    sub x1 -> x0, other arithmetic: 1.44 us -> none  [per_device(): new_slowness = slowness - update_rate * normed]
    pallas_call x1, Pallas kernels: 49.8 us -> 50.6 us  [per_device(): pl.pallas_call(functools.partial(kernel, shots, slabs), name='invert', ou...]
    dynamic_slice x1 -> x0, local copies, waits for them, and re-layouts: 0.65 us -> none  [per_device(): lax.dynamic_slice_in_dim(normed, lax.axis_index('shot') * share, share, 1)]
where the time goes in v2:
time: 53.4 us; the launch traced here: 53.2 us
  Pallas kernels  52.6 us (99%)
  between operations  0.64 us (1%)
    pallas_call x1, Pallas kernels, per_device(): pl.pallas_call(functools.partial(kernel, shots, slabs), name='invert', ou...  50.6 us
    pallas_call x1, Pallas kernels, per_device(): pl.pallas_call(finish, name='finish', out_shape=(jax.ShapeDtypeStruct(blo...  1.95 us

profile of v2, /device:TPU:0, one launch (start us, length us, event | category | flops | bytes accessed | tf_op | source)
XLA Modules:
  0.0 53.2 jit_solution(3289721131552863047)
XLA Ops:
  0.6 50.6 %invert.1 = (f32[4,192,128]{2,1,0:T(8,128)}, f32[8,128]{1,0:T(8,128)}) custom-call(f32[4,192,128]{2,1,0:T(8,128)} %slowness.1, f32[1,4,192,128]{3,2,1,0:T(8,128)} %prev_in.1, f32[1,4,192,128]{3,2,1,0:T(8,128)} %now_in.1, f32[1,3,4,192,128]{4,3,2,1,0:T(8,128)} %memory_in.1, f32[1,4,192,128]{3,2,1,0:T(8,128)} %adj_now_in.1, f32[1,4,192,128]{3,2,1,0:T(8,128)} %adj_prev_in.1, ...), custom_call_target="tpu_custom_call" | custom-call | tf_op jit(solution)/shard_map/invert/pallas_call | solution.py:476
  51.3 2.0 %finish.1 = (f32[4,192,128]{2,1,0:T(8,128)}, f32[4,48,128]{2,1,0:T(8,128)}) custom-call(f32[4,192,128]{2,1,0:T(8,128)} %get-tuple-element.4.total, f32[4,192,128]{2,1,0:T(8,128)} %slowness.1, f32[8,128]{1,0:T(8,128)} %get-tuple-element.5.inverse), custom_call_target="tpu_custom_call" | custom-call | tf_op jit(solution)/shard_map/finish/pallas_call | solution.py:536

commit v3 on v2

--- a/solution.py
+++ b/solution.py
@@ -11,8 +11,8 @@
 MECH = 3
 LINK = 2
 PAD = 8
-CHUNKS = 4
-SUB = 24
+CHUNKS = 6
+SUB = 16
 
 center_coef = -2.5
 near_coef = 4.0 / 3.0

time: 53.4 us -> 55.6 us (1.041)
  Pallas kernels: 52.6 us -> 54.8 us
    pallas_call x1, Pallas kernels: 50.6 us -> 52.8 us  [per_device(): pl.pallas_call(functools.partial(kernel, shots, slabs), name='invert', ou...]
where the time goes in v3:
time: 55.6 us; the launch traced here: 55.4 us
  Pallas kernels  54.8 us (99%)
  between operations  0.64 us (1%)
    pallas_call x1, Pallas kernels, per_device(): pl.pallas_call(functools.partial(kernel, shots, slabs), name='invert', ou...  52.8 us
    pallas_call x1, Pallas kernels, per_device(): pl.pallas_call(finish, name='finish', out_shape=(jax.ShapeDtypeStruct(blo...  1.95 us

profile of v3, /device:TPU:0, one launch (start us, length us, event | category | flops | bytes accessed | tf_op | source)
XLA Modules:
  0.0 55.4 jit_solution(2607974851072807527)
XLA Ops:
  0.6 52.8 %invert.1 = (f32[4,192,128]{2,1,0:T(8,128)}, f32[8,128]{1,0:T(8,128)}) custom-call(f32[4,192,128]{2,1,0:T(8,128)} %slowness.1, f32[1,4,192,128]{3,2,1,0:T(8,128)} %prev_in.1, f32[1,4,192,128]{3,2,1,0:T(8,128)} %now_in.1, f32[1,3,4,192,128]{4,3,2,1,0:T(8,128)} %memory_in.1, f32[1,4,192,128]{3,2,1,0:T(8,128)} %adj_now_in.1, f32[1,4,192,128]{3,2,1,0:T(8,128)} %adj_prev_in.1, ...), custom_call_target="tpu_custom_call" | custom-call | tf_op jit(solution)/shard_map/invert/pallas_call | solution.py:476
  53.4 2.0 %finish.1 = (f32[4,192,128]{2,1,0:T(8,128)}, f32[4,48,128]{2,1,0:T(8,128)}) custom-call(f32[4,192,128]{2,1,0:T(8,128)} %get-tuple-element.4.total, f32[4,192,128]{2,1,0:T(8,128)} %slowness.1, f32[8,128]{1,0:T(8,128)} %get-tuple-element.5.inverse), custom_call_target="tpu_custom_call" | custom-call | tf_op jit(solution)/shard_map/finish/pallas_call | solution.py:536

commit v4 on v2

--- a/solution.py
+++ b/solution.py
@@ -22,6 +22,10 @@
 relax_weight = (0.3, 0.2, 0.1)
 update_rate = 0.05
 tiny_eps = 1e-06
+
+lag_weight = tuple(
+    sum(w * a**j for w, a in zip(relax_weight, relax_decay)) for j in range(STEPS - 1)
+)
 
 MESH = pl.DeviceIdType.MESH
 
@@ -55,7 +59,9 @@
     drive,
     united,
     saved,
-    back_relax,
+    fading,
+    curves,
+    pushes,
     accum,
     scaled,
     factor,
@@ -69,6 +75,7 @@
     parts,
     total,
     squares,
+    sums,
     load_sem,
     halo_send,
     halo_recv,
@@ -78,6 +85,8 @@
     whole_recv,
     square_send,
     square_recv,
+    sum_send,
+    sum_recv,
 ):
     depth, width, lanes = slow.shape
     rows = width // CHUNKS
@@ -215,7 +224,19 @@
         held = courant / (s * s)
         scaled[d] = held
         factor[d] = (-2.0 * held) / s
-    for k in (0, 2, 3, 4, 5):
+    loads[2].wait()
+
+    def fade(k, carry):
+        at = pl.ds(pl.multiple_of(k * SUB, 8), SUB)
+        for d in range(depth):
+            held = [relax[m, d, at] for m in range(MECH)]
+            for n in range(STEPS):
+                fading[n, d, at] = (held[0] + held[1]) + held[2]
+                held = [relax_decay[m] * held[m] for m in range(MECH)]
+        return carry
+
+    lax.fori_loop(0, width // SUB, fade, 0)
+    for k in (0, 3, 4, 5):
         loads[k].wait()
 
     lane = lax.broadcasted_iota(jnp.int32, (8, lanes), 1)[:1]
@@ -266,14 +287,13 @@
         united[level, d, at] = up
         pushed = scaled[d, at] * up
         out = pushed
-        for m in range(MECH):
-            if begin_accum:
-                back_relax[m, d, at] = pushed
-            else:
-                held = back_relax[m, d, at]
-                out = out - relax_weight[m] * held
-                if level > 1:
-                    back_relax[m, d, at] = relax_decay[m] * held + pushed
+        if level == STEPS - 2:
+            pushes[d, at] = pushed
+            out = pushed - lag_weight[0] * drive[0, d, pl.ds(r + PAD, SUB)]
+        elif level == STEPS - 3:
+            out = (pushed - lag_weight[0] * pushes[d, at]) - lag_weight[1] * drive[
+                0, d, pl.ds(r + PAD, SUB)
+            ]
         drive[STEPS - 1 - level, d, pl.ds(r + PAD, SUB)] = out
 
     def forward_stage(n):
@@ -289,18 +309,16 @@
                 inner = pl.ds(r + PAD, SUB)
                 curved, mids = laplace(field, n, n, r)
                 for d in range(depth):
-                    held = [relax[m, d, at] for m in range(MECH)]
-                    accel = curved[d] + ((held[0] + held[1]) + held[2])
+                    accel = curved[d] + fading[n, d, at]
+                    for m in range(n):
+                        accel = accel - lag_weight[n - 1 - m] * curves[m, d, at]
                     before = older[d, at] if n == 0 else field[n - 1, d, inner]
                     newer = (2.0 * mids[d] - before) + scaled[d, at] * accel
                     newer = newer + amount * source[d, at]
                     saved[n, d, at] = accel
                     field[n + 1, d, inner] = newer
                     if n < STEPS - 1:
-                        for m in range(MECH):
-                            relax[m, d, at] = (
-                                relax_decay[m] * held[m] - relax_weight[m] * curved[d]
-                            )
+                        curves[n, d, at] = curved[d]
                     else:
                         adjoint_part(n, d, r, adj_now[d, at], True)
 
@@ -395,22 +413,11 @@
     for c in range(CHUNKS - 2, CHUNKS):
         reduce_chunk(c)
 
-    def settle(c, carry):
-        wait_sent(stages - 1, c)
-        for k in range(1, shots):
-            part_copy(k, c).wait_send()
-            whole_copy(k, c).wait()
-        return carry
-
-    lax.fori_loop(0, CHUNKS, settle, 0)
-
-    store = pltpu.make_async_copy(total, total_out, load_sem.at[0])
-    store.start()
-
     summed = jnp.zeros((8, lanes), jnp.float32)
-    for d in range(depth):
-        block = total[d]
-        summed = summed + jnp.sum((block * block).reshape(width // 8, 8, lanes), axis=0)
+    for c in range(CHUNKS):
+        d, r = spot(shot, c)
+        held = total[d, pl.ds(r, piece)]
+        summed = summed + jnp.sum((held * held).reshape(piece // 8, 8, lanes), axis=0)
     squares[me] = summed
 
     def square_copy(k):
@@ -423,13 +430,50 @@
             device_id_type=MESH,
         )
 
+    def shot_copy(k):
+        return pltpu.make_async_remote_copy(
+            src_ref=sums.at[shot],
+            dst_ref=sums.at[shot],
+            send_sem=sum_send.at[k - 1],
+            recv_sem=sum_recv.at[k - 1],
+            device_id={"shot": lax.rem(shot + k, shots)},
+            device_id_type=MESH,
+        )
+
     for k in range(1, slabs):
         square_copy(k).start()
+
+    def settle_parts(c, carry):
+        wait_sent(stages - 1, c)
+        for k in range(1, shots):
+            part_copy(k, c).wait_send()
+        return carry
+
+    lax.fori_loop(0, CHUNKS, settle_parts, 0)
     for k in range(1, slabs):
-        square_copy(k).wait()
+        square_copy(k).wait_recv()
     everything = squares[0]
     for k in range(1, slabs):
         everything = everything + squares[k]
+    sums[shot] = everything
+    for k in range(1, shots):
+        shot_copy(k).start()
+
+    def settle(c, carry):
+        for k in range(1, shots):
+            whole_copy(k, c).wait()
+        return carry
+
+    lax.fori_loop(0, CHUNKS, settle, 0)
+    store = pltpu.make_async_copy(total, total_out, load_sem.at[0])
+    store.start()
+    for k in range(1, slabs):
+        square_copy(k).wait_send()
+    for k in range(1, shots):
+        shot_copy(k).wait()
+    everything = sums[0]
+    for k in range(1, shots):
+        everything = everything + sums[k]
     cells = slabs * depth * width * lanes
     mean = jnp.sum(everything, keepdims=True) / cells + tiny_eps
     inv_out[...] = jnp.broadcast_to(1.0 / jnp.sqrt(mean), inv_out.shape)
@@ -492,7 +536,9 @@
             pltpu.VMEM((STEPS - 1, *padded), f32),
             pltpu.VMEM((STEPS, *block), f32),
             pltpu.VMEM((STEPS, *block), f32),
-            pltpu.VMEM((MECH, *block), f32),
+            pltpu.VMEM((STEPS, *block), f32),
+            pltpu.VMEM((STEPS - 1, *block), f32),
+            pltpu.VMEM(block, f32),
             pltpu.VMEM(block, f32),
             pltpu.VMEM(block, f32),
             pltpu.VMEM(block, f32),
@@ -506,6 +552,7 @@
             pltpu.VMEM((CHUNKS, shots - 1, piece, lanes), f32),
             pltpu.VMEM(block, f32),
             pltpu.VMEM((slabs, 8, lanes), f32),
+            pltpu.VMEM((shots, 8, lanes), f32),
             dma((6,)),
             dma((stages, 2, CHUNKS)),
             dma((stages, 2, CHUNKS)),
@@ -515,6 +562,8 @@
             dma((CHUNKS, shots - 1)),
             dma((slabs - 1,)),
             dma((slabs - 1,)),
+            dma((shots - 1,)),
+            dma((shots - 1,)),
         ],
         compiler_params=pltpu.CompilerParams(
             collective_id=0, has_side_effects=True, vmem_limit_bytes=60 * 2**20

time: 53.4 us -> 53 us (level)
  no operation moved by 1% of the time
where the time goes in v4:
time: 53 us; the launch traced here: 52.8 us
  Pallas kernels  52.2 us (98%)
  between operations  0.64 us (1%)
    pallas_call x1, Pallas kernels, per_device(): pl.pallas_call(functools.partial(kernel, shots, slabs), name='invert', ou...  50.2 us
    pallas_call x1, Pallas kernels, per_device(): pl.pallas_call(finish, name='finish', out_shape=(jax.ShapeDtypeStruct(blo...  1.95 us

profile of v4, /device:TPU:0, one launch (start us, length us, event | category | flops | bytes accessed | tf_op | source)
XLA Modules:
  0.0 52.8 jit_solution(13860719552326773294)
XLA Ops:
  0.6 50.2 %invert.1 = (f32[4,192,128]{2,1,0:T(8,128)}, f32[8,128]{1,0:T(8,128)}) custom-call(f32[4,192,128]{2,1,0:T(8,128)} %slowness.1, f32[1,4,192,128]{3,2,1,0:T(8,128)} %prev_in.1, f32[1,4,192,128]{3,2,1,0:T(8,128)} %now_in.1, f32[1,3,4,192,128]{4,3,2,1,0:T(8,128)} %memory_in.1, f32[1,4,192,128]{3,2,1,0:T(8,128)} %adj_now_in.1, f32[1,4,192,128]{3,2,1,0:T(8,128)} %adj_prev_in.1, ...), custom_call_target="tpu_custom_call" | custom-call | tf_op jit(solution)/shard_map/invert/pallas_call | solution.py:520
  50.9 2.0 %finish.1 = (f32[4,192,128]{2,1,0:T(8,128)}, f32[4,48,128]{2,1,0:T(8,128)}) custom-call(f32[4,192,128]{2,1,0:T(8,128)} %get-tuple-element.4.total, f32[4,192,128]{2,1,0:T(8,128)} %slowness.1, f32[8,128]{1,0:T(8,128)} %get-tuple-element.5.inverse), custom_call_target="tpu_custom_call" | custom-call | tf_op jit(solution)/shard_map/finish/pallas_call | solution.py:585

commit v5 on v4

--- a/solution.py
+++ b/solution.py
@@ -11,8 +11,8 @@
 MECH = 3
 LINK = 2
 PAD = 8
-CHUNKS = 4
-SUB = 24
+CHUNKS = 3
+SUB = 32
 
 center_coef = -2.5
 near_coef = 4.0 / 3.0
@@ -43,11 +43,11 @@
     memory_in,
     adj_now_in,
     adj_prev_in,
-    wavelet,
-    src_cells,
-    src_signs,
-    rec_cells,
-    observed,
+    wavelet_in,
+    src_cells_in,
+    src_signs_in,
+    rec_cells_in,
+    observed_in,
     total_out,
     inv_out,
     slow,
@@ -76,6 +76,11 @@
     total,
     squares,
     sums,
+    wavelet,
+    src_cells,
+    src_signs,
+    rec_cells,
+    observed,
     load_sem,
     halo_send,
     halo_recv,
@@ -101,6 +106,11 @@
         pltpu.make_async_copy(prev_in.at[0], older, load_sem.at[3]),
         pltpu.make_async_copy(adj_now_in.at[0], adj_now, load_sem.at[4]),
         pltpu.make_async_copy(adj_prev_in.at[0], adj_prev, load_sem.at[5]),
+        pltpu.make_async_copy(wavelet_in, wavelet, load_sem.at[6]),
+        pltpu.make_async_copy(src_cells_in, src_cells, load_sem.at[7]),
+        pltpu.make_async_copy(src_signs_in, src_signs, load_sem.at[8]),
+        pltpu.make_async_copy(rec_cells_in, rec_cells, load_sem.at[9]),
+        pltpu.make_async_copy(observed_in, observed, load_sem.at[10]),
     ]
     barrier = pltpu.get_barrier_semaphore()
     for k in range(1, slabs):
@@ -189,6 +199,8 @@
         return jnp.where(at == index, 1.0, 0.0)
 
     first_row = me * (depth * width)
+    for k in range(6, 11):
+        loads[k].wait()
     src = src_cells[...]
     src_row = lax.div(src, lanes)
     src_lane = src - src_row * lanes
@@ -515,7 +527,6 @@
     padded = (depth, width + 2 * PAD, lanes)
     anywhere = pl.BlockSpec(memory_space=pl.ANY)
     vmem = pl.BlockSpec(memory_space=pltpu.VMEM)
-    smem = pl.BlockSpec(memory_space=pltpu.SMEM)
     dma = pltpu.SemaphoreType.DMA
     total, inverse = pl.pallas_call(
         functools.partial(kernel, shots, slabs),
@@ -524,7 +535,7 @@
             jax.ShapeDtypeStruct(block, f32),
             jax.ShapeDtypeStruct((8, lanes), f32),
         ),
-        in_specs=[anywhere] * 6 + [smem] + [vmem] * 4,
+        in_specs=[anywhere] * 11,
         out_specs=(anywhere, vmem),
         scratch_shapes=[
             pltpu.VMEM(block, f32),
@@ -553,7 +564,12 @@
             pltpu.VMEM(block, f32),
             pltpu.VMEM((slabs, 8, lanes), f32),
             pltpu.VMEM((shots, 8, lanes), f32),
-            dma((6,)),
+            pltpu.SMEM(wavelet.shape, f32),
+            pltpu.VMEM(src_cells.shape, jnp.int32),
+            pltpu.VMEM(src_signs.shape, jnp.int32),
+            pltpu.VMEM((1, receivers), jnp.int32),
+            pltpu.VMEM(observed.shape, f32),
+            dma((11,)),
             dma((stages, 2, CHUNKS)),
             dma((stages, 2, CHUNKS)),
             dma((CHUNKS, shots - 1)),

time: 53 us -> 50.6 us (0.955)
  Pallas kernels: 52.2 us -> 49.8 us
    pallas_call x1, Pallas kernels: 50.2 us -> 47.9 us  [per_device(): pl.pallas_call(functools.partial(kernel, shots, slabs), name='invert', ou...]
where the time goes in v5:
time: 50.6 us; the launch traced here: 50.5 us
  Pallas kernels  49.8 us (98%)
  between operations  0.64 us (1%)
    pallas_call x1, Pallas kernels, per_device(): pl.pallas_call(functools.partial(kernel, shots, slabs), name='invert', ou...  47.9 us
    pallas_call x1, Pallas kernels, per_device(): pl.pallas_call(finish, name='finish', out_shape=(jax.ShapeDtypeStruct(blo...  1.95 us

profile of v5, /device:TPU:0, one launch (start us, length us, event | category | flops | bytes accessed | tf_op | source)
XLA Modules:
  0.0 50.5 jit_solution(14379662183047550398)
XLA Ops:
  0.6 47.9 %invert.1 = (f32[4,192,128]{2,1,0:T(8,128)}, f32[8,128]{1,0:T(8,128)}) custom-call(f32[4,192,128]{2,1,0:T(8,128)} %slowness.1, f32[1,4,192,128]{3,2,1,0:T(8,128)} %prev_in.1, f32[1,4,192,128]{3,2,1,0:T(8,128)} %now_in.1, f32[1,3,4,192,128]{4,3,2,1,0:T(8,128)} %memory_in.1, f32[1,4,192,128]{3,2,1,0:T(8,128)} %adj_now_in.1, f32[1,4,192,128]{3,2,1,0:T(8,128)} %adj_prev_in.1, ...), custom_call_target="tpu_custom_call" | custom-call | tf_op jit(solution)/shard_map/invert/pallas_call | solution.py:531
  48.5 2.0 %finish.1 = (f32[4,192,128]{2,1,0:T(8,128)}, f32[4,48,128]{2,1,0:T(8,128)}) custom-call(f32[4,192,128]{2,1,0:T(8,128)} %get-tuple-element.4.total, f32[4,192,128]{2,1,0:T(8,128)} %slowness.1, f32[8,128]{1,0:T(8,128)} %get-tuple-element.5.inverse), custom_call_target="tpu_custom_call" | custom-call | tf_op jit(solution)/shard_map/finish/pallas_call | solution.py:601

commit v6 on v5

--- a/solution.py
+++ b/solution.py
@@ -11,8 +11,8 @@
 MECH = 3
 LINK = 2
 PAD = 8
-CHUNKS = 3
-SUB = 32
+CHUNKS = 4
+WIDE = 2
 
 center_coef = -2.5
 near_coef = 4.0 / 3.0
@@ -96,6 +96,7 @@
     depth, width, lanes = slow.shape
     rows = width // CHUNKS
     stages = 2 * STEPS - 1
+    cuts = [WIDE] * (stages - 1) + [CHUNKS]
     me = lax.axis_index("slab")
     shot = lax.axis_index("shot")
 
@@ -128,17 +129,18 @@
     def outgoing(stage, side, c):
         first = depth - LINK if side == 0 else 0
         planes = pl.ds(first, LINK)
-        start = pl.multiple_of(c * rows, 8)
+        span = width // cuts[stage]
+        start = pl.multiple_of(c * span, 8)
         if stage == 0:
-            src = now_in.at[0, planes, pl.ds(start, rows)]
+            src = now_in.at[0, planes, pl.ds(start, span)]
         elif stage < STEPS:
-            src = field.at[stage, planes, pl.ds(start + PAD, rows)]
+            src = field.at[stage, planes, pl.ds(start + PAD, span)]
         else:
-            src = drive.at[stage - STEPS, planes, pl.ds(start + PAD, rows)]
+            src = drive.at[stage - STEPS, planes, pl.ds(start + PAD, span)]
         target = me + 1 if side == 0 else me - 1
         return pltpu.make_async_remote_copy(
             src_ref=src,
-            dst_ref=halo.at[stage, side, :, pl.ds(start, rows)],
+            dst_ref=halo.at[stage, side, :, pl.ds(start, span)],
             send_sem=halo_send.at[stage, side, c],
             recv_sem=halo_recv.at[stage, side, c],
             device_id={"slab": target},
@@ -148,6 +150,11 @@
     has_up = me < slabs - 1
     has_down = me > 0
 
+    def send_after(stage, c):
+        ratio = cuts[stage + 1] // cuts[stage]
+        for k in range(ratio):
+            send_halo(stage + 1, c * ratio + k)
+
     def send_halo(stage, c):
         @pl.when(has_up)
         def _():
@@ -175,7 +182,7 @@
         def _():
             outgoing(stage, 1, c).wait_recv()
 
-    for c in range(CHUNKS):
+    for c in range(cuts[0]):
         send_halo(0, c)
 
     @pl.when(jnp.logical_not(has_down))
@@ -239,7 +246,7 @@
     loads[2].wait()
 
     def fade(k, carry):
-        at = pl.ds(pl.multiple_of(k * SUB, 8), SUB)
+        at = pl.ds(pl.multiple_of(k * 24, 8), 24)
         for d in range(depth):
             held = [relax[m, d, at] for m in range(MECH)]
             for n in range(STEPS):
@@ -247,7 +254,7 @@
                 held = [relax_decay[m] * held[m] for m in range(MECH)]
         return carry
 
-    lax.fori_loop(0, width // SUB, fade, 0)
+    lax.fori_loop(0, width // 24, fade, 0)
     for k in (0, 3, 4, 5):
         loads[k].wait()
 
@@ -257,13 +264,13 @@
     right_1 = jnp.where(lane < lanes - 1, near_coef, 0.0)
     right_2 = jnp.where(lane < lanes - 2, far_coef, 0.0)
 
-    def laplace(ref, n, stage, r):
+    def laplace(ref, n, stage, r, size):
         def rows_at(d, shift):
-            return ref[n, d, pl.ds(r + PAD + shift, SUB)]
-
-        low = [halo[stage, 0, k, pl.ds(r, SUB)] for k in range(LINK)]
+            return ref[n, d, pl.ds(r + PAD + shift, size)]
+
+        low = [halo[stage, 0, k, pl.ds(r, size)] for k in range(LINK)]
         mids = [rows_at(d, 0) for d in range(depth)]
-        high = [halo[stage, 1, k, pl.ds(r, SUB)] for k in range(LINK)]
+        high = [halo[stage, 1, k, pl.ds(r, size)] for k in range(LINK)]
         planes = low + mids + high
         curved = []
         for d in range(depth):
@@ -281,14 +288,17 @@
             )
         return curved, mids
 
-    def blocks(c, body):
-        for k in range(rows // SUB):
-            body(pl.multiple_of(c * rows + k * SUB, 8))
-
-    def adjoint_part(level, d, r, back, begin_accum):
-        at = pl.ds(r, SUB)
+    def blocks(stage, c, body):
+        span = width // cuts[stage]
+        size = 32 if span % 32 == 0 else 24 if span % 24 == 0 else 8
+        for k in range(span // size):
+            body(pl.multiple_of(c * span + k * size, 8), size)
+
+    def adjoint_part(level, d, r, size, back, begin_accum):
+        at = pl.ds(r, size)
+        inner = pl.ds(r + PAD, size)
         up = back + (
-            count[d, at] * field[level + 1, d, pl.ds(r + PAD, SUB)] - seen[level, d, at]
+            count[d, at] * field[level + 1, d, inner] - seen[level, d, at]
         )
         term = up * saved[level, d, at]
         term = term if begin_accum else accum[d, at] + term
@@ -301,25 +311,23 @@
         out = pushed
         if level == STEPS - 2:
             pushes[d, at] = pushed
-            out = pushed - lag_weight[0] * drive[0, d, pl.ds(r + PAD, SUB)]
+            out = pushed - lag_weight[0] * drive[0, d, inner]
         elif level == STEPS - 3:
             out = (pushed - lag_weight[0] * pushes[d, at]) - lag_weight[1] * drive[
-                0, d, pl.ds(r + PAD, SUB)
+                0, d, inner
             ]
-        drive[STEPS - 1 - level, d, pl.ds(r + PAD, SUB)] = out
+        drive[STEPS - 1 - level, d, inner] = out
 
     def forward_stage(n):
         amount = wavelet[n]
 
         def chunk(c, carry):
             wait_halo(n, c)
-            if n > 0:
-                wait_sent(n - 1, c)
-
-            def body(r):
-                at = pl.ds(r, SUB)
-                inner = pl.ds(r + PAD, SUB)
-                curved, mids = laplace(field, n, n, r)
+
+            def body(r, size):
+                at = pl.ds(r, size)
+                inner = pl.ds(r + PAD, size)
+                curved, mids = laplace(field, n, n, r, size)
                 for d in range(depth):
                     accel = curved[d] + fading[n, d, at]
                     for m in range(n):
@@ -332,13 +340,13 @@
                     if n < STEPS - 1:
                         curves[n, d, at] = curved[d]
                     else:
-                        adjoint_part(n, d, r, adj_now[d, at], True)
-
-            blocks(c, body)
-            send_halo(n + 1, c)
+                        adjoint_part(n, d, r, size, adj_now[d, at], True)
+
+            blocks(n, c, body)
+            send_after(n, c)
             return carry
 
-        lax.fori_loop(0, CHUNKS, chunk, 0)
+        lax.fori_loop(0, cuts[n], chunk, 0)
 
     piece = depth * rows // shots
 
@@ -385,22 +393,21 @@
 
         def chunk(c, carry):
             wait_halo(stage, c)
-            wait_sent(stage - 1, c)
-
-            def body(r):
-                at = pl.ds(r, SUB)
-                curved, _ = laplace(drive, stage - STEPS, stage, r)
+
+            def body(r, size):
+                at = pl.ds(r, size)
+                curved, _ = laplace(drive, stage - STEPS, stage, r, size)
                 for d in range(depth):
                     after = united[level + 1, d, at]
                     if level == STEPS - 2:
                         base = adj_prev[d, at]
                     else:
                         base = -united[level + 2, d, at]
-                    adjoint_part(level, d, r, (base + 2.0 * after) + curved[d], False)
-
-            blocks(c, body)
+                    adjoint_part(level, d, r, size, (base + 2.0 * after) + curved[d], False)
+
+            blocks(stage, c, body)
             if level > 0:
-                send_halo(stage + 1, c)
+                send_after(stage, c)
             else:
                 for k in range(1, shots):
                     part_copy(k, c).start()
@@ -411,7 +418,7 @@
 
             return carry
 
-        lax.fori_loop(0, CHUNKS, chunk, 0)
+        lax.fori_loop(0, cuts[stage], chunk, 0)
 
     for n in range(STEPS):
         forward_stage(n)
@@ -456,12 +463,14 @@
         square_copy(k).start()
 
     def settle_parts(c, carry):
-        wait_sent(stages - 1, c)
         for k in range(1, shots):
             part_copy(k, c).wait_send()
         return carry
 
     lax.fori_loop(0, CHUNKS, settle_parts, 0)
+    for stage in range(stages):
+        for c in range(cuts[stage]):
+            wait_sent(stage, c)
     for k in range(1, slabs):
         square_copy(k).wait_recv()
     everything = squares[0]
@@ -492,13 +501,51 @@
     store.wait()
 
 
-def finish(total, slowness, inverse, new_slowness, gradient):
-    share = gradient.shape[1]
+def finish(
+    total_in,
+    slowness_in,
+    inverse_in,
+    new_slowness_out,
+    gradient_out,
+    total,
+    slowness,
+    inverse,
+    new_slowness,
+    gradient,
+    scale_sem,
+    total_sem,
+    slow_sem,
+    new_sem,
+    grad_sem,
+):
+    depth, share = gradient.shape[:2]
     first = pl.multiple_of(lax.axis_index("shot") * share, 8)
+    scale = pltpu.make_async_copy(inverse_in, inverse, scale_sem)
+    scale.start()
+    loads = []
+    for d in range(depth):
+        loads.append(
+            (
+                pltpu.make_async_copy(total_in.at[d], total.at[d], total_sem.at[d]),
+                pltpu.make_async_copy(slowness_in.at[d], slowness.at[d], slow_sem.at[d]),
+            )
+        )
+        for copy in loads[d]:
+            copy.start()
+    scale.wait()
     inv = inverse[0:1]
-    for d in range(total.shape[0]):
+    stores = []
+    for d in range(depth):
+        for copy in loads[d]:
+            copy.wait()
         new_slowness[d] = slowness[d] - update_rate * (total[d] * inv)
         gradient[d] = total[d, pl.ds(first, share)] * inv
+        stores.append(pltpu.make_async_copy(new_slowness.at[d], new_slowness_out.at[d], new_sem.at[d]))
+        stores.append(pltpu.make_async_copy(gradient.at[d], gradient_out.at[d], grad_sem.at[d]))
+        for copy in stores[-2:]:
+            copy.start()
+    for copy in stores:
+        copy.wait()
 
 
 def per_device(
@@ -518,7 +565,7 @@
     shots, slabs = lax.axis_size("shot"), lax.axis_size("slab")
     rows = width // CHUNKS
     piece = depth * rows // shots
-    assert width % CHUNKS == 0 and rows % SUB == 0 and depth >= LINK
+    assert width % 96 == 0 and depth >= LINK
     assert depth * rows % shots == 0 and rows % piece == 0 and piece % 8 == 0
     receivers = rec_cells.shape[0]
     stages = 2 * STEPS - 1
@@ -605,8 +652,20 @@
             jax.ShapeDtypeStruct(block, f32),
             jax.ShapeDtypeStruct((depth, share, lanes), f32),
         ),
-        in_specs=[vmem] * 3,
-        out_specs=(vmem, vmem),
+        in_specs=[anywhere] * 3,
+        out_specs=(anywhere, anywhere),
+        scratch_shapes=[
+            pltpu.VMEM(block, f32),
+            pltpu.VMEM(block, f32),
+            pltpu.VMEM((8, lanes), f32),
+            pltpu.VMEM(block, f32),
+            pltpu.VMEM((depth, share, lanes), f32),
+            dma(()),
+            dma((depth,)),
+            dma((depth,)),
+            dma((depth,)),
+            dma((depth,)),
+        ],
         compiler_params=pltpu.CompilerParams(vmem_limit_bytes=60 * 2**20),
     )(total, slowness, inverse)
     return (new_slowness, gradient)

time: 50.6 us -> 55.3 us (1.093)
  Pallas kernels: 49.8 us -> 54.5 us
    pallas_call x1, Pallas kernels: 47.9 us -> 52.4 us  [per_device(): pl.pallas_call(functools.partial(kernel, shots, slabs), name='invert', ou...]
where the time goes in v6:
time: 55.3 us; the launch traced here: 55.1 us
  Pallas kernels  54.5 us (99%)
  between operations  0.64 us (1%)
    pallas_call x1, Pallas kernels, per_device(): pl.pallas_call(functools.partial(kernel, shots, slabs), name='invert', ou...  52.4 us
    pallas_call x1, Pallas kernels, per_device(): pl.pallas_call(finish, name='finish', out_shape=(jax.ShapeDtypeStruct(blo...  2.03 us

profile of v6, /device:TPU:0, one launch (start us, length us, event | category | flops | bytes accessed | tf_op | source)
XLA Modules:
  0.0 55.1 jit_solution(11102617880336666189)
XLA Ops:
  0.6 52.4 %invert.1 = (f32[4,192,128]{2,1,0:T(8,128)}, f32[8,128]{1,0:T(8,128)}) custom-call(f32[4,192,128]{2,1,0:T(8,128)} %slowness_in.3, f32[1,4,192,128]{3,2,1,0:T(8,128)} %prev_in.1, f32[1,4,192,128]{3,2,1,0:T(8,128)} %now_in.1, f32[1,3,4,192,128]{4,3,2,1,0:T(8,128)} %memory_in.1, f32[1,4,192,128]{3,2,1,0:T(8,128)} %adj_now_in.1, f32[1,4,192,128]{3,2,1,0:T(8,128)} %adj_prev_in.1, ...), custom_call_target="tpu_custom_call" | custom-call | tf_op jit(solution)/shard_map/invert/pallas_call | solution.py:578
  53.1 2.0 %finish.1 = (f32[4,192,128]{2,1,0:T(8,128)}, f32[4,48,128]{2,1,0:T(8,128)}) custom-call(f32[4,192,128]{2,1,0:T(8,128)} %get-tuple-element.4.total_in, f32[4,192,128]{2,1,0:T(8,128)} %slowness_in.3, f32[8,128]{1,0:T(8,128)} %get-tuple-element.5.inverse_in), custom_call_target="tpu_custom_call" | custom-call | tf_op jit(solution)/shard_map/finish/pallas_call | solution.py:648

commit v7 on v6

--- a/solution.py
+++ b/solution.py
@@ -11,8 +11,9 @@
 MECH = 3
 LINK = 2
 PAD = 8
-CHUNKS = 4
-WIDE = 2
+CHUNKS = 6
+LAG = 4
+WIDE = 3
 
 center_coef = -2.5
 near_coef = 4.0 / 3.0
@@ -75,7 +76,6 @@
     parts,
     total,
     squares,
-    sums,
     wavelet,
     src_cells,
     src_signs,
@@ -90,8 +90,6 @@
     whole_recv,
     square_send,
     square_recv,
-    sum_send,
-    sum_recv,
 ):
     depth, width, lanes = slow.shape
     rows = width // CHUNKS
@@ -114,17 +112,21 @@
         pltpu.make_async_copy(observed_in, observed, load_sem.at[10]),
     ]
     barrier = pltpu.get_barrier_semaphore()
-    for k in range(1, slabs):
-        pl.semaphore_signal(
-            barrier, inc=1, device_id={"slab": lax.rem(me + k, slabs)}, device_id_type=MESH
-        )
-    for k in range(1, shots):
-        pl.semaphore_signal(
-            barrier, inc=1, device_id={"shot": lax.rem(shot + k, shots)}, device_id_type=MESH
-        )
+    team = shots * slabs
+    place = me * shots + shot
+
+    def member(k):
+        other = lax.rem(place + k, team)
+        return {"slab": other // shots, "shot": lax.rem(other, shots)}
+
+    def greet(k, carry):
+        pl.semaphore_signal(barrier, inc=1, device_id=member(k), device_id_type=MESH)
+        return carry
+
+    lax.fori_loop(1, team, greet, 0)
     for copy in loads:
         copy.start()
-    pl.semaphore_wait(barrier, slabs - 1 + shots - 1)
+    pl.semaphore_wait(barrier, team - 1)
 
     def outgoing(stage, side, c):
         first = depth - LINK if side == 0 else 0
@@ -231,11 +233,12 @@
         hot_rows[...] = one_hot(rec_row - first_row, depth * width).astype(jnp.bfloat16)
         count[...] = contract_lanes(hot_rows[...], pieces[0:lanes]).reshape(depth, width, lanes)
 
-    def place_observed(n):
+    def place_observed(n, part, parts_of):
+        height = depth * width // parts_of
+        at = pl.ds(pl.multiple_of(part * height, 16), height)
         begin = (1 + 3 * n) * lanes
-        got = contract_lanes(hot_rows[...], pieces[begin : begin + 3 * lanes])
-        got = (got[:, 2 * lanes :] + got[:, lanes : 2 * lanes]) + got[:, :lanes]
-        seen[n] = got.reshape(depth, width, lanes)
+        got = contract_lanes(hot_rows[at], pieces[begin : begin + 3 * lanes])
+        seen[n, at] = (got[:, 2 * lanes :] + got[:, lanes : 2 * lanes]) + got[:, :lanes]
 
     loads[1].wait()
     for d in range(depth):
@@ -255,6 +258,8 @@
         return carry
 
     lax.fori_loop(0, width // 24, fade, 0)
+    place_receivers()
+    place_observed(STEPS - 1, 0, 1)
     for k in (0, 3, 4, 5):
         loads[k].wait()
 
@@ -298,7 +303,7 @@
         at = pl.ds(r, size)
         inner = pl.ds(r + PAD, size)
         up = back + (
-            count[d, at] * field[level + 1, d, inner] - seen[level, d, at]
+            count[d, at] * field[level + 1, d, inner] - seen[level, pl.ds(d * width + r, size)]
         )
         term = up * saved[level, d, at]
         term = term if begin_accum else accum[d, at] + term
@@ -344,6 +349,8 @@
 
             blocks(n, c, body)
             send_after(n, c)
+            if n < STEPS - 1:
+                place_observed(STEPS - 2 - n, c, cuts[n])
             return carry
 
         lax.fori_loop(0, cuts[n], chunk, 0)
@@ -412,9 +419,9 @@
                 for k in range(1, shots):
                     part_copy(k, c).start()
 
-                @pl.when(c >= 2)
+                @pl.when(c >= LAG)
                 def _():
-                    reduce_chunk(c - 2)
+                    reduce_chunk(c - LAG)
 
             return carry
 
@@ -422,14 +429,9 @@
 
     for n in range(STEPS):
         forward_stage(n)
-        if n == 0:
-            place_receivers()
-        if n in (1, 2):
-            for k in (2 * n - 2, 2 * n - 1):
-                place_observed(k)
     for level in reversed(range(STEPS - 1)):
         backward_stage(level)
-    for c in range(CHUNKS - 2, CHUNKS):
+    for c in range(CHUNKS - LAG, CHUNKS):
         reduce_chunk(c)
 
     summed = jnp.zeros((8, lanes), jnp.float32)
@@ -437,30 +439,23 @@
         d, r = spot(shot, c)
         held = total[d, pl.ds(r, piece)]
         summed = summed + jnp.sum((held * held).reshape(piece // 8, 8, lanes), axis=0)
-    squares[me] = summed
+    squares[place] = summed
 
     def square_copy(k):
         return pltpu.make_async_remote_copy(
-            src_ref=squares.at[me],
-            dst_ref=squares.at[me],
+            src_ref=squares.at[place],
+            dst_ref=squares.at[place],
             send_sem=square_send.at[k - 1],
             recv_sem=square_recv.at[k - 1],
-            device_id={"slab": lax.rem(me + k, slabs)},
+            device_id=member(k),
             device_id_type=MESH,
         )
 
-    def shot_copy(k):
-        return pltpu.make_async_remote_copy(
-            src_ref=sums.at[shot],
-            dst_ref=sums.at[shot],
-            send_sem=sum_send.at[k - 1],
-            recv_sem=sum_recv.at[k - 1],
-            device_id={"shot": lax.rem(shot + k, shots)},
-            device_id_type=MESH,
-        )
-
-    for k in range(1, slabs):
+    def tell(k, carry):
         square_copy(k).start()
+        return carry
+
+    lax.fori_loop(1, team, tell, 0)
 
     def settle_parts(c, carry):
         for k in range(1, shots):
@@ -471,15 +466,6 @@
     for stage in range(stages):
         for c in range(cuts[stage]):
             wait_sent(stage, c)
-    for k in range(1, slabs):
-        square_copy(k).wait_recv()
-    everything = squares[0]
-    for k in range(1, slabs):
-        everything = everything + squares[k]
-    sums[shot] = everything
-    for k in range(1, shots):
-        shot_copy(k).start()
-
     def settle(c, carry):
         for k in range(1, shots):
             whole_copy(k, c).wait()
@@ -488,64 +474,26 @@
     lax.fori_loop(0, CHUNKS, settle, 0)
     store = pltpu.make_async_copy(total, total_out, load_sem.at[0])
     store.start()
-    for k in range(1, slabs):
-        square_copy(k).wait_send()
-    for k in range(1, shots):
-        shot_copy(k).wait()
-    everything = sums[0]
-    for k in range(1, shots):
-        everything = everything + sums[k]
+
+    def hear(k, carry):
+        square_copy(k).wait()
+        return carry
+
+    lax.fori_loop(1, team, hear, 0)
+    everything = jnp.sum(squares[...], axis=0)
     cells = slabs * depth * width * lanes
     mean = jnp.sum(everything, keepdims=True) / cells + tiny_eps
     inv_out[...] = jnp.broadcast_to(1.0 / jnp.sqrt(mean), inv_out.shape)
     store.wait()
 
 
-def finish(
-    total_in,
-    slowness_in,
-    inverse_in,
-    new_slowness_out,
-    gradient_out,
-    total,
-    slowness,
-    inverse,
-    new_slowness,
-    gradient,
-    scale_sem,
-    total_sem,
-    slow_sem,
-    new_sem,
-    grad_sem,
-):
-    depth, share = gradient.shape[:2]
+def finish(total, slowness, inverse, new_slowness, gradient):
+    share = gradient.shape[1]
     first = pl.multiple_of(lax.axis_index("shot") * share, 8)
-    scale = pltpu.make_async_copy(inverse_in, inverse, scale_sem)
-    scale.start()
-    loads = []
-    for d in range(depth):
-        loads.append(
-            (
-                pltpu.make_async_copy(total_in.at[d], total.at[d], total_sem.at[d]),
-                pltpu.make_async_copy(slowness_in.at[d], slowness.at[d], slow_sem.at[d]),
-            )
-        )
-        for copy in loads[d]:
-            copy.start()
-    scale.wait()
     inv = inverse[0:1]
-    stores = []
-    for d in range(depth):
-        for copy in loads[d]:
-            copy.wait()
+    for d in range(total.shape[0]):
         new_slowness[d] = slowness[d] - update_rate * (total[d] * inv)
         gradient[d] = total[d, pl.ds(first, share)] * inv
-        stores.append(pltpu.make_async_copy(new_slowness.at[d], new_slowness_out.at[d], new_sem.at[d]))
-        stores.append(pltpu.make_async_copy(gradient.at[d], gradient_out.at[d], grad_sem.at[d]))
-        for copy in stores[-2:]:
-            copy.start()
-    for copy in stores:
-        copy.wait()
 
 
 def per_device(
@@ -601,7 +549,7 @@
             pltpu.VMEM(block, f32),
             pltpu.VMEM(block, f32),
             pltpu.VMEM(block, f32),
-            pltpu.VMEM((STEPS, *block), f32),
+            pltpu.VMEM((STEPS, depth * width, lanes), f32),
             pltpu.VMEM(block, f32),
             pltpu.VMEM((depth * width, receivers), jnp.bfloat16),
             pltpu.VMEM(((1 + 3 * STEPS) * lanes, receivers), jnp.bfloat16),
@@ -609,8 +557,7 @@
             pltpu.VMEM(block, f32),
             pltpu.VMEM((CHUNKS, shots - 1, piece, lanes), f32),
             pltpu.VMEM(block, f32),
-            pltpu.VMEM((slabs, 8, lanes), f32),
-            pltpu.VMEM((shots, 8, lanes), f32),
+            pltpu.VMEM((shots * slabs, 8, lanes), f32),
             pltpu.SMEM(wavelet.shape, f32),
             pltpu.VMEM(src_cells.shape, jnp.int32),
             pltpu.VMEM(src_signs.shape, jnp.int32),
@@ -623,10 +570,8 @@
             dma((CHUNKS, shots - 1)),
             dma((CHUNKS, shots - 1)),
             dma((CHUNKS, shots - 1)),
-            dma((slabs - 1,)),
-            dma((slabs - 1,)),
-            dma((shots - 1,)),
-            dma((shots - 1,)),
+            dma((shots * slabs - 1,)),
+            dma((shots * slabs - 1,)),
         ],
         compiler_params=pltpu.CompilerParams(
             collective_id=0, has_side_effects=True, vmem_limit_bytes=60 * 2**20
@@ -652,20 +597,8 @@
             jax.ShapeDtypeStruct(block, f32),
             jax.ShapeDtypeStruct((depth, share, lanes), f32),
         ),
-        in_specs=[anywhere] * 3,
-        out_specs=(anywhere, anywhere),
-        scratch_shapes=[
-            pltpu.VMEM(block, f32),
-            pltpu.VMEM(block, f32),
-            pltpu.VMEM((8, lanes), f32),
-            pltpu.VMEM(block, f32),
-            pltpu.VMEM((depth, share, lanes), f32),
-            dma(()),
-            dma((depth,)),
-            dma((depth,)),
-            dma((depth,)),
-            dma((depth,)),
-        ],
+        in_specs=[vmem] * 3,
+        out_specs=(vmem, vmem),
         compiler_params=pltpu.CompilerParams(vmem_limit_bytes=60 * 2**20),
     )(total, slowness, inverse)
     return (new_slowness, gradient)

time: 55.3 us -> 51.9 us (0.939)
  Pallas kernels: 54.5 us -> 51.1 us
    pallas_call x1, Pallas kernels: 52.4 us -> 49.1 us  [per_device(): pl.pallas_call(functools.partial(kernel, shots, slabs), name='invert', ou...]
where the time goes in v7:
time: 51.9 us; the launch traced here: 51.7 us
  Pallas kernels  51.1 us (98%)
  between operations  0.64 us (1%)
    pallas_call x1, Pallas kernels, per_device(): pl.pallas_call(functools.partial(kernel, shots, slabs), name='invert', ou...  49.1 us
    pallas_call x1, Pallas kernels, per_device(): pl.pallas_call(finish, name='finish', out_shape=(jax.ShapeDtypeStruct(blo...  1.95 us

profile of v7, /device:TPU:0, one launch (start us, length us, event | category | flops | bytes accessed | tf_op | source)
XLA Modules:
  0.0 51.7 jit_solution(7473242861510921395)
XLA Ops:
  0.6 49.1 %invert.1 = (f32[4,192,128]{2,1,0:T(8,128)}, f32[8,128]{1,0:T(8,128)}) custom-call(f32[4,192,128]{2,1,0:T(8,128)} %slowness.1, f32[1,4,192,128]{3,2,1,0:T(8,128)} %prev_in.1, f32[1,4,192,128]{3,2,1,0:T(8,128)} %now_in.1, f32[1,3,4,192,128]{4,3,2,1,0:T(8,128)} %memory_in.1, f32[1,4,192,128]{3,2,1,0:T(8,128)} %adj_now_in.1, f32[1,4,192,128]{3,2,1,0:T(8,128)} %adj_prev_in.1, ...), custom_call_target="tpu_custom_call" | custom-call | tf_op jit(solution)/shard_map/invert/pallas_call | solution.py:526
  49.8 2.0 %finish.1 = (f32[4,192,128]{2,1,0:T(8,128)}, f32[4,48,128]{2,1,0:T(8,128)}) custom-call(f32[4,192,128]{2,1,0:T(8,128)} %get-tuple-element.4.total, f32[4,192,128]{2,1,0:T(8,128)} %slowness.1, f32[8,128]{1,0:T(8,128)} %get-tuple-element.5.inverse), custom_call_target="tpu_custom_call" | custom-call | tf_op jit(solution)/shard_map/finish/pallas_call | solution.py:593

commit v8 on v5

--- a/solution.py
+++ b/solution.py
@@ -224,11 +224,12 @@
         hot_rows[...] = one_hot(rec_row - first_row, depth * width).astype(jnp.bfloat16)
         count[...] = contract_lanes(hot_rows[...], pieces[0:lanes]).reshape(depth, width, lanes)
 
-    def place_observed(n):
+    def place_observed(n, part, parts_of):
+        height = depth * width // parts_of
+        at = pl.ds(pl.multiple_of(part * height, 16), height)
         begin = (1 + 3 * n) * lanes
-        got = contract_lanes(hot_rows[...], pieces[begin : begin + 3 * lanes])
-        got = (got[:, 2 * lanes :] + got[:, lanes : 2 * lanes]) + got[:, :lanes]
-        seen[n] = got.reshape(depth, width, lanes)
+        got = contract_lanes(hot_rows[at], pieces[begin : begin + 3 * lanes])
+        seen[n, at] = (got[:, 2 * lanes :] + got[:, lanes : 2 * lanes]) + got[:, :lanes]
 
     loads[1].wait()
     for d in range(depth):
@@ -250,6 +251,8 @@
     lax.fori_loop(0, width // SUB, fade, 0)
     for k in (0, 3, 4, 5):
         loads[k].wait()
+    place_receivers()
+    place_observed(STEPS - 1, 0, 1)
 
     lane = lax.broadcasted_iota(jnp.int32, (8, lanes), 1)[:1]
     left_1 = jnp.where(lane >= 1, near_coef, 0.0)
@@ -288,7 +291,7 @@
     def adjoint_part(level, d, r, back, begin_accum):
         at = pl.ds(r, SUB)
         up = back + (
-            count[d, at] * field[level + 1, d, pl.ds(r + PAD, SUB)] - seen[level, d, at]
+            count[d, at] * field[level + 1, d, pl.ds(r + PAD, SUB)] - seen[level, pl.ds(d * width + r, SUB)]
         )
         term = up * saved[level, d, at]
         term = term if begin_accum else accum[d, at] + term
@@ -336,6 +339,8 @@
 
             blocks(c, body)
             send_halo(n + 1, c)
+            if n < STEPS - 1:
+                place_observed(STEPS - 2 - n, c, CHUNKS)
             return carry
 
         lax.fori_loop(0, CHUNKS, chunk, 0)
@@ -415,11 +420,6 @@
 
     for n in range(STEPS):
         forward_stage(n)
-        if n == 0:
-            place_receivers()
-        if n in (1, 2):
-            for k in (2 * n - 2, 2 * n - 1):
-                place_observed(k)
     for level in reversed(range(STEPS - 1)):
         backward_stage(level)
     for c in range(CHUNKS - 2, CHUNKS):
@@ -554,7 +554,7 @@
             pltpu.VMEM(block, f32),
             pltpu.VMEM(block, f32),
             pltpu.VMEM(block, f32),
-            pltpu.VMEM((STEPS, *block), f32),
+            pltpu.VMEM((STEPS, depth * width, lanes), f32),
             pltpu.VMEM(block, f32),
             pltpu.VMEM((depth * width, receivers), jnp.bfloat16),
             pltpu.VMEM(((1 + 3 * STEPS) * lanes, receivers), jnp.bfloat16),

time: 50.6 us -> 50.6 us (level)
  no operation moved by 1% of the time
where the time goes in v8:
time: 50.6 us; the launch traced here: 50.5 us
  Pallas kernels  49.8 us (98%)
  between operations  0.64 us (1%)
    pallas_call x1, Pallas kernels, per_device(): pl.pallas_call(functools.partial(kernel, shots, slabs), name='invert', ou...  47.9 us
    pallas_call x1, Pallas kernels, per_device(): pl.pallas_call(finish, name='finish', out_shape=(jax.ShapeDtypeStruct(blo...  1.95 us

profile of v8, /device:TPU:0, one launch (start us, length us, event | category | flops | bytes accessed | tf_op | source)
XLA Modules:
  0.0 50.5 jit_solution(13886753722969090063)
XLA Ops:
  0.6 47.9 %invert.1 = (f32[4,192,128]{2,1,0:T(8,128)}, f32[8,128]{1,0:T(8,128)}) custom-call(f32[4,192,128]{2,1,0:T(8,128)} %slowness.1, f32[1,4,192,128]{3,2,1,0:T(8,128)} %prev_in.1, f32[1,4,192,128]{3,2,1,0:T(8,128)} %now_in.1, f32[1,3,4,192,128]{4,3,2,1,0:T(8,128)} %memory_in.1, f32[1,4,192,128]{3,2,1,0:T(8,128)} %adj_now_in.1, f32[1,4,192,128]{3,2,1,0:T(8,128)} %adj_prev_in.1, ...), custom_call_target="tpu_custom_call" | custom-call | tf_op jit(solution)/shard_map/invert/pallas_call | solution.py:531
  48.5 2.0 %finish.1 = (f32[4,192,128]{2,1,0:T(8,128)}, f32[4,48,128]{2,1,0:T(8,128)}) custom-call(f32[4,192,128]{2,1,0:T(8,128)} %get-tuple-element.4.total, f32[4,192,128]{2,1,0:T(8,128)} %slowness.1, f32[8,128]{1,0:T(8,128)} %get-tuple-element.5.inverse), custom_call_target="tpu_custom_call" | custom-call | tf_op jit(solution)/shard_map/finish/pallas_call | solution.py:601
